TPU v7x, 32 devices: a whole 2x2x4 slice. The times are simulated.
32 devices in a mesh: hst: 4 (over y, x), dev: 8 (over z, core).
Axes of the slice: x: 2, y: 2, z: 4, core: 2. Of those that a mesh axis runs over, the one named last changes fastest.
Arguments:
- replay: bfloat16 [4096, 28224], P(('hst', 'dev')), may hold values from 0 to 1
- send_index: int32 [32, 32, 8], P(('hst', 'dev')), may hold values from 0 to 127
- send_count: int32 [32, 32], P(('hst', 'dev')), may hold values from 0 to 8, as said below
- actions: int32 [32, 32, 8], P(('hst', 'dev')), may hold values from 0 to 17
- game_ids: int32 [32, 32, 8], P(('hst', 'dev')), may hold values from 0 to 56
- legal_table: int32 [57, 18], replicated, may hold values 0 or 1
- returns: float32 [32, 32, 8], P(('hst', 'dev')), may hold values from -6 to 6
- bootstrap: float32 [32, 32, 8], P(('hst', 'dev')), may hold values from -6 to 6
- is_weights: float32 [32, 32, 8], P(('hst', 'dev')), may hold values from 0.1 to 1
- priority_table: float32 [4096], P(('hst', 'dev')), may hold values from 0.3 to 3
- conv1_w: bfloat16 [8, 8, 4, 32], replicated, may hold values from -0.375 to 0.375
- conv1_b: bfloat16 [32], replicated, may hold values from -1.5 to 1.5
- conv2_w: bfloat16 [4, 4, 32, 64], replicated, may hold values from -0.25 to 0.25
- conv2_b: bfloat16 [64], replicated, may hold values from -1.5 to 1.5
- conv3_w: bfloat16 [3, 3, 64, 64], replicated, may hold values from -0.25 to 0.25
- conv3_b: bfloat16 [64], replicated, may hold values from -1.5 to 1.5
- dense_w: bfloat16 [3136, 512], replicated, may hold values from -0.109375 to 0.109375
- dense_b: bfloat16 [512], replicated, may hold values from -1.5 to 1.5
- value_w: bfloat16 [512, 1], replicated, may hold values from -0.25 to 0.25
- value_b: bfloat16 [1], replicated, may hold values from -1.5 to 1.5
- advantage_w: bfloat16 [512, 18], replicated, may hold values from -0.25 to 0.25
- advantage_b: bfloat16 [18], replicated, may hold values from -1.5 to 1.5
Outputs:
- q_values: float32 [32, 256, 18], P(('hst', 'dev'))
- loss: float32 [], replicated
- grad_conv1_w: float32 [8, 8, 4, 32], replicated
- grad_conv1_b: float32 [32], replicated
- grad_conv2_w: float32 [4, 4, 32, 64], replicated
- grad_conv2_b: float32 [64], replicated
- grad_conv3_w: float32 [3, 3, 64, 64], replicated
- grad_conv3_b: float32 [64], replicated
- grad_dense_w: float32 [3136, 512], replicated
- grad_dense_b: float32 [512], replicated
- grad_value_w: float32 [512, 1], replicated
- grad_value_b: float32 [1], replicated
- grad_advantage_w: float32 [512, 18], replicated
- grad_advantage_b: float32 [18], replicated
- new_table: float32 [4096], P(('hst', 'dev'))
- top_priority: float32 [], replicated
Inputs may be any that keep to these rules, and one draw needn't show every extreme that they name: `send_count`: in every draw one learner receives 8 live slots from every owner.
All inputs are finite; a program needn't handle non-finite values.
Results may differ from a plain program's by a relative error of at most 0.0021.
Values may be sent and summed in bfloat16 or wider, within the bound.
A program may use at most 192 MiB of HBM per device.

v0:
```python
import jax
import jax.numpy as jnp
from jax import lax
from jax.sharding import PartitionSpec as P

FRAME = 84
STACK = 4
S1 = 4
S2 = 2
S3 = 1


GAMMA_THREE = 0.970299
PLAIN_SPEC = ("NHWC", "HWIO", "NHWC")


def forward_conv(source, kernel, stride):
    return lax.conv_general_dilated(
        source,
        kernel,
        (stride, stride),
        "VALID",
        dimension_numbers=PLAIN_SPEC,
        preferred_element_type=jnp.float32,
    )


def kernel_grad(source, upstream, stride):
    return lax.conv_general_dilated(
        source,
        upstream,
        (1, 1),
        "VALID",
        rhs_dilation=(stride, stride),
        dimension_numbers=("CHWN", "IHWO", "HWNC"),
        preferred_element_type=jnp.float32,
    )


def source_grad(upstream, kernel, stride):
    margin = kernel.shape[0] - 1
    return lax.conv_general_dilated(
        upstream,
        jnp.flip(kernel, (0, 1)),
        (1, 1),
        ((margin, margin), (margin, margin)),
        lhs_dilation=(stride, stride),
        dimension_numbers=("NHWC", "HWOI", "NHWC"),
        preferred_element_type=jnp.float32,
    )


def silu_slope(pre_value):
    gate_value = jax.nn.sigmoid(pre_value)
    return gate_value * (1.0 + pre_value * (1.0 - gate_value))


def huber(td_error):
    magnitude = jnp.abs(td_error)
    return jnp.where(magnitude <= 1.0, 0.5 * td_error * td_error, magnitude - 0.5)


def transposed_dot(left_side, right_side):
    return lax.dot_general(
        left_side, right_side, (((0,), (0,)), ((), ())), preferred_element_type=jnp.float32
    )


def learn(frames, live_rows, action_ids, game_rows, target_rows, weight_rows, legal_table, params):
    (
        conv1_w,
        conv1_b,
        conv2_w,
        conv2_b,
        conv3_w,
        conv3_b,
        dense_w,
        dense_b,
        value_w,
        value_b,
        advantage_w,
        advantage_b,
    ) = params
    total_rows = frames.shape[0]
    block_rows = min(128, total_rows)
    block_count = total_rows // block_rows
    head_w = jnp.concatenate([value_w, advantage_w], 1)
    head_b = jnp.concatenate([value_b, advantage_b], 0).astype(jnp.float32)
    game_count = legal_table.shape[0]
    action_count = legal_table.shape[1]
    noop_mask = (jnp.arange(action_count) == 0).astype(jnp.float32)
    legal_rows = jnp.maximum(legal_table.astype(jnp.float32), noop_mask[None, :])

    def one_block(running, pieces):
        accumulated, loss_sum = running
        frame_part, live_part, action_part, game_part, target_part, weight_part = pieces
        row_count = frame_part.shape[0]
        pictures = frame_part.reshape(row_count, FRAME, FRAME, STACK)
        pre_one = forward_conv(pictures, conv1_w, S1) + conv1_b.astype(jnp.float32)
        act_one = jax.nn.silu(pre_one).astype(jnp.bfloat16)
        pre_two = forward_conv(act_one, conv2_w, S2) + conv2_b.astype(jnp.float32)
        act_two = jax.nn.silu(pre_two).astype(jnp.bfloat16)
        pre_three = forward_conv(act_two, conv3_w, S3) + conv3_b.astype(jnp.float32)
        act_three = jax.nn.silu(pre_three).astype(jnp.bfloat16)
        flat_three = act_three.reshape(row_count, -1)
        pre_dense = jnp.dot(
            flat_three, dense_w, preferred_element_type=jnp.float32
        ) + dense_b.astype(jnp.float32)
        act_dense = jax.nn.silu(pre_dense).astype(jnp.bfloat16)
        head_out = jnp.dot(act_dense, head_w, preferred_element_type=jnp.float32) + head_b
        state_value = head_out[:, :1]
        advantage = head_out[:, 1:]
        game_pick = (game_part[:, None] == jnp.arange(game_count)[None, :]).astype(jnp.float32)
        legal_mask = jnp.dot(game_pick, legal_rows, precision=lax.Precision.HIGHEST)
        counted = jnp.sum(legal_mask, 1)
        centre = jnp.sum(advantage * legal_mask, 1) / counted
        q_part = state_value + advantage - centre[:, None]
        act_pick = (action_part[:, None] == jnp.arange(action_count)[None, :]).astype(jnp.float32)
        td_error = target_part - jnp.sum(q_part * act_pick, 1)
        scaled = live_part * weight_part
        loss_sum = loss_sum + jnp.sum(scaled * huber(td_error)) / total_rows
        grad_taken = -scaled * jnp.clip(td_error, -1.0, 1.0) / total_rows
        grad_q = grad_taken[:, None] * act_pick
        grad_value = jnp.sum(grad_q, 1, keepdims=True)
        grad_adv = grad_q - legal_mask * (jnp.sum(grad_q, 1) / counted)[:, None]
        grad_head = jnp.concatenate([grad_value, grad_adv], 1).astype(jnp.bfloat16)
        head_w_grad = transposed_dot(act_dense, grad_head)
        head_b_grad = jnp.sum(grad_head.astype(jnp.float32), 0)
        up_dense = lax.dot_general(
            grad_head, head_w, (((1,), (1,)), ((), ())), preferred_element_type=jnp.float32
        )
        grad_dense = (up_dense * silu_slope(pre_dense)).astype(jnp.bfloat16)
        dense_w_grad = transposed_dot(flat_three, grad_dense)
        dense_b_grad = jnp.sum(grad_dense.astype(jnp.float32), 0)
        up_three = lax.dot_general(
            grad_dense, dense_w, (((1,), (1,)), ((), ())), preferred_element_type=jnp.float32
        ).reshape(act_three.shape)
        grad_three = (up_three * silu_slope(pre_three)).astype(jnp.bfloat16)
        conv3_w_grad = kernel_grad(act_two, grad_three, S3)
        conv3_b_grad = jnp.sum(grad_three.astype(jnp.float32), (0, 1, 2))
        up_two = source_grad(grad_three, conv3_w, S3)
        grad_two = (up_two * silu_slope(pre_two)).astype(jnp.bfloat16)
        conv2_w_grad = kernel_grad(act_one, grad_two, S2)
        conv2_b_grad = jnp.sum(grad_two.astype(jnp.float32), (0, 1, 2))
        up_one = source_grad(grad_two, conv2_w, S2)
        grad_one = (up_one * silu_slope(pre_one)).astype(jnp.bfloat16)
        conv1_w_grad = kernel_grad(pictures, grad_one, S1)
        conv1_b_grad = jnp.sum(grad_one.astype(jnp.float32), (0, 1, 2))
        fresh_terms = (
            conv1_w_grad,
            conv1_b_grad,
            conv2_w_grad,
            conv2_b_grad,
            conv3_w_grad,
            conv3_b_grad,
            dense_w_grad,
            dense_b_grad,
            head_w_grad[:, :1],
            head_b_grad[:1],
            head_w_grad[:, 1:],
            head_b_grad[1:],
        )
        accumulated = tuple((before + after for before, after in zip(accumulated, fresh_terms)))
        return ((accumulated, loss_sum), (q_part, td_error))

    starting = tuple((jnp.zeros(piece.shape, jnp.float32) for piece in params))
    pieces = (
        frames.reshape(block_count, block_rows, -1),
        live_rows.reshape(block_count, block_rows),
        action_ids.reshape(block_count, block_rows),
        game_rows.reshape(block_count, block_rows),
        target_rows.reshape(block_count, block_rows),
        weight_rows.reshape(block_count, block_rows),
    )
    (accumulated, loss_sum), (q_blocks, td_blocks) = lax.scan(
        one_block, (starting, jnp.zeros((), jnp.float32)), pieces
    )
    return (q_blocks.reshape(total_rows, -1), td_blocks.reshape(total_rows), loss_sum, accumulated)


def per_device(
    replay,
    send_index,
    send_count,
    actions,
    game_ids,
    legal_table,
    returns,
    bootstrap,
    is_weights,
    priority_table,
    conv1_w,
    conv1_b,
    conv2_w,
    conv2_b,
    conv3_w,
    conv3_b,
    dense_w,
    dense_b,
    value_w,
    value_b,
    advantage_w,
    advantage_b,
):
    params = (
        conv1_w,
        conv1_b,
        conv2_w,
        conv2_b,
        conv3_w,
        conv3_b,
        dense_w,
        dense_b,
        value_w,
        value_b,
        advantage_w,
        advantage_b,
    )
    peer_count = lax.axis_size(("hst", "dev"))
    capacity = send_index.shape[2]
    pixel_count = replay.shape[1]
    own_index = send_index[0]
    own_live = jnp.arange(capacity, dtype=jnp.int32)[None, :] < send_count[0][:, None]
    packed = jnp.take(replay, own_index.reshape(-1), axis=0).reshape(
        peer_count, capacity, pixel_count
    )
    live_mark = own_live.astype(jnp.bfloat16)
    arrived, arrived_live = (
        lax.all_to_all(packed, ("hst", "dev"), split_axis=0, concat_axis=0, tiled=True),
        lax.all_to_all(live_mark, ("hst", "dev"), split_axis=0, concat_axis=0, tiled=True),
    )
    frames = arrived.reshape(peer_count * capacity, pixel_count)
    live_rows = arrived_live.reshape(-1).astype(jnp.float32)
    target_rows = (returns[0] + GAMMA_THREE * bootstrap[0]).reshape(-1)
    q_rows, td_rows, loss_local, grads = learn(
        frames,
        live_rows,
        actions[0].reshape(-1),
        game_ids[0].reshape(-1),
        target_rows,
        is_weights[0].reshape(-1),
        legal_table,
        params,
    )
    q_values = q_rows.reshape(1, peer_count * capacity, -1)
    returned = lax.all_to_all(
        ((td_rows * td_rows + 1.0) ** 0.3).reshape(peer_count, capacity),
        ("hst", "dev"),
        split_axis=0,
        concat_axis=0,
        tiled=True,
    )
    totals = lax.psum(
        (
            loss_local,
            grads[0],
            grads[1],
            grads[2],
            grads[3],
            grads[4],
            grads[5],
            grads[6],
            grads[7],
            grads[8],
            grads[9],
            grads[10],
            grads[11],
        ),
        ("hst", "dev"),
    )
    candidates = jnp.where(own_live, returned, 0.0).reshape(-1)
    fresh = jnp.zeros(priority_table.shape, jnp.float32).at[own_index.reshape(-1)].max(candidates)
    new_table = jnp.where(fresh > 0.0, fresh, priority_table)
    top_priority = lax.pmax(jnp.max(new_table), ("hst", "dev"))
    return (
        q_values,
        totals[0],
        totals[1],
        totals[2],
        totals[3],
        totals[4],
        totals[5],
        totals[6],
        totals[7],
        totals[8],
        totals[9],
        totals[10],
        totals[11],
        totals[12],
        new_table,
        top_priority,
    )


def solution(mesh):
    placed = (
        P(("hst", "dev"), None),
        P(("hst", "dev"), None, None),
        P(("hst", "dev"), None),
        P(("hst", "dev"), None, None),
        P(("hst", "dev"), None, None),
        P(),
        P(("hst", "dev"), None, None),
        P(("hst", "dev"), None, None),
        P(("hst", "dev"), None, None),
        P(("hst", "dev")),
        P(),
        P(),
        P(),
        P(),
        P(),
        P(),
        P(),
        P(),
        P(),
        P(),
        P(),
        P(),
    )
    return jax.shard_map(
        per_device,
        mesh=mesh,
        in_specs=placed,
        out_specs=(
            P(("hst", "dev"), None, None),
            P(),
            P(),
            P(),
            P(),
            P(),
            P(),
            P(),
            P(),
            P(),
            P(),
            P(),
            P(),
            P(),
            P(("hst", "dev")),
            P(),
        ),
        check_vma=False,
    )
```

profile of v0, /device:TPU:1, one launch (start us, length us, event | category | flops | bytes accessed | tf_op | source)
XLA Modules:
  0.0 770.1 jit_solution(8401851828813330692)
XLA Ops:
  7.2 1.4 compare_convert_fusion
  8.5 7.1 all-to-all-start.1
  16.3 0.8 copy.55
  17.3 10.4 %copy.56 = bf16[128,28224]{1,0:T(8,128)(2,1)} copy(bf16[128,28224]{0,1:T(8,128)(2,1)} %param.24) | data formatting | bytes 14450688 | tf_op args[0]
  27.7 31.6 %gather_fusion = bf16[256,28224]{1,0:T(8,128)(2,1)} fusion(bf16[128,28224]{1,0:T(8,128)(2,1)} %copy.56, s32[1024]{0:T(1024)S(1)} %pad_clamp_fusion), kind=kCustom, calls=%fused_computation | custom fusion | bytes 28902400 | tf_op jit(solution)/shard_map/jit(_take)/gather | solution.py:224
  59.3 13.4 %bitcast_select_fusion = bf16[32,8,28224]{2,1,0:T(8,128)(2,1)} fusion(bf16[256,28224]{1,0:T(8,128)(2,1)} %gather_fusion, pred[32,8]{1,0:T(8,128)(4,1)S(1)} %copy.54), kind=kLoop, calls=%fused_computation.71 | loop fusion | flops 7225344 | bytes 28901632 | tf_op jit(solution)/shard_map/jit(_take)/select_n | solution.py:224
  72.7 5.9 all-to-all-start
  84.3 309.3 %all-to-all-done = bf16[32,8,28224]{2,1,0:T(8,128)(2,1)} async-done(((bf16[32,8,28224]{2,1,0:T(8,128)(2,1)}), bf16[32,8,28224]{2,1,0:T(8,128)(2,1)}, u32[]{:S(2)}, u32[]{:S(2)}) %all-to-all-start) | async-done | bytes 14450720 | tf_op jit(solution)/shard_map/all_to_all | solution.py:229
  393.6 19.8 %copy.61 = bf16[2,128,28224]{1,2,0:T(8,128)(2,1)} copy(bf16[2,128,28224]{2,1,0:T(8,128)(2,1)} %bitcast.3) | data formatting | bytes 28901376
  413.4 175.6 %while.41 = (s32[]{:T(128)}, f32[8,8,4,32]{3,2,1,0:T(4,128)}, f32[32]{0:T(128)}, f32[4,4,32,64]{3,2,1,0:T(8,128)}, f32[64]{0:T(128)}, /*index=5*/f32[3,3,64,64]{...) while((s32[]{:T(128)}, f32[8,8,4,32]{3,2,1,0:T(4,128)}, ...), condition=%wide.region_11.12_spmd.clone, body=%wide.region_0.11_spmd.clone.sunk | while | flops 6398834176 | bytes 253833616 | solution.py:175
  436.7 6.5 constant_dynamic-slice_fusion.7
  443.1 13.8 %multiply_convert_fusion.12 = (bf16[128,20,20,32]{0,3,2,1:T(8,128)(2,1)S(1)}, f32[128,20,20,32]{0,3,2,1:T(8,128)}) fusion(f32[32]{0:T(128)S(1)} %convert_element_type.219, bf16[128,84,84,4]{0,3,2,1:T(4,128)(2,1)} %bitcast.146, bf16[8,8,4,32]{3,2,1,0:T(4,128)(2,1)} %get-tuple-element.1068), kind=kOutput, calls=%fused_computation.5.clone.1 | convolution fusion | flops 848691200 | bytes 17072256 | tf_op jit(solution)/shard_map/while/body/eval_jaxpr/conv_general_dilated | solution.py:18
  456.9 4.3 multiply_convert_fusion.13
  461.2 3.7 multiply_convert_fusion.14
  464.9 0.9 copy-done.2
  465.9 1.3 multiply_convert_fusion.15
  467.2 0.8 convolution_add_fusion.11
  468.0 1.0 fusion.115
  469.2 1.3 dynamic_update_slice.19
  470.4 1.2 multiply_reduce_fusion.3
  472.3 1.2 convert_reduce_fusion.11
  474.5 1.4 dynamic_update_slice.18
  475.9 1.0 fusion.119
  477.3 0.9 convert_reduce_fusion.12
  478.7 3.8 convert_reduce_fusion.13
  482.6 2.1 convolution_add_fusion.14
  484.7 8.2 %convert_reduce_fusion.14 = (f32[32]{0:T(128)S(1)}, bf16[128,20,20,32]{0,3,2,1:T(8,128)(2,1)S(1)}) fusion(f32[128,20,20,32]{0,3,2,1:T(8,128)S(1)} %bitcast.160, f32[32]{0:T(128)S(1)} %copy-done.35, bf16[128,9,9,64]{0,3,2,1:T(8,128)(2,1)S(1)} %get-tuple-element.965, bf16[4,4,32,64]{3,2,1,0:T(8,128)(2,1)} %get-tuple-element.1070), kind=kOutput, calls=%fused_computation.3.clone.1 | convolution fusion | flops 699138048 | bytes 11223296 | tf_op jit(solution)/shard_map/while/body/eval_jaxpr/conv_general_dilated | solution.py:42
  492.9 2.9 convolution_add_fusion.13
  496.0 9.9 %convolution_add_fusion.12 = f32[8,8,4,32]{3,2,1,0:T(4,128)S(1)} fusion(bf16[128,84,84,4]{0,3,2,1:T(4,128)(2,1)S(1)} %bitcast.149, bf16[128,20,20,32]{0,3,2,1:T(8,128)(2,1)S(1)} %get-tuple-element.966, f32[8,8,4,32]{3,2,1,0:T(4,128)S(1)} %copy-done.9, pred[]{:T(512)S(6)} %compare.3), kind=kOutput, calls=%fused_computation.20.clone.1 | convolution fusion | flops 838877184 | bytes 10567681 | tf_op jit(solution)/shard_map/while/body/eval_jaxpr/conv_general_dilated | solution.py:29
  506.0 1.9 convolution_add_fusion.15
  508.0 2.7 copy-done.1
  514.1 6.5 constant_dynamic-slice_fusion.7
  520.5 13.8 %multiply_convert_fusion.12 = (bf16[128,20,20,32]{0,3,2,1:T(8,128)(2,1)S(1)}, f32[128,20,20,32]{0,3,2,1:T(8,128)}) fusion(f32[32]{0:T(128)S(1)} %convert_element_type.219, bf16[128,84,84,4]{0,3,2,1:T(4,128)(2,1)} %bitcast.146, bf16[8,8,4,32]{3,2,1,0:T(4,128)(2,1)} %get-tuple-element.1068), kind=kOutput, calls=%fused_computation.5.clone.1 | convolution fusion | flops 848691200 | bytes 17072256 | tf_op jit(solution)/shard_map/while/body/eval_jaxpr/conv_general_dilated | solution.py:18
  534.3 4.3 multiply_convert_fusion.13
  538.6 3.7 multiply_convert_fusion.14
  542.3 0.9 copy-done.2
  543.3 1.3 multiply_convert_fusion.15
  544.6 0.8 convolution_add_fusion.11
  545.4 1.0 fusion.115
  546.5 1.3 dynamic_update_slice.19
  547.8 1.2 multiply_reduce_fusion.3
  549.7 1.2 convert_reduce_fusion.11
  551.3 1.2 fusion.124
  552.5 1.4 dynamic_update_slice.18
  553.9 1.0 fusion.119
  555.3 0.9 convert_reduce_fusion.12
  556.8 3.8 convert_reduce_fusion.13
  560.6 2.1 convolution_add_fusion.14
  562.8 8.2 %convert_reduce_fusion.14 = (f32[32]{0:T(128)S(1)}, bf16[128,20,20,32]{0,3,2,1:T(8,128)(2,1)S(1)}) fusion(f32[128,20,20,32]{0,3,2,1:T(8,128)S(1)} %bitcast.160, f32[32]{0:T(128)S(1)} %copy-done.35, bf16[128,9,9,64]{0,3,2,1:T(8,128)(2,1)S(1)} %get-tuple-element.965, bf16[4,4,32,64]{3,2,1,0:T(8,128)(2,1)} %get-tuple-element.1070), kind=kOutput, calls=%fused_computation.3.clone.1 | convolution fusion | flops 699138048 | bytes 11223296 | tf_op jit(solution)/shard_map/while/body/eval_jaxpr/conv_general_dilated | solution.py:42
  571.0 2.9 convolution_add_fusion.13
  574.0 9.9 %convolution_add_fusion.12 = f32[8,8,4,32]{3,2,1,0:T(4,128)S(1)} fusion(bf16[128,84,84,4]{0,3,2,1:T(4,128)(2,1)S(1)} %bitcast.149, bf16[128,20,20,32]{0,3,2,1:T(8,128)(2,1)S(1)} %get-tuple-element.966, f32[8,8,4,32]{3,2,1,0:T(4,128)S(1)} %copy-done.9, pred[]{:T(512)S(6)} %compare.3), kind=kOutput, calls=%fused_computation.20.clone.1 | convolution fusion | flops 838877184 | bytes 10567681 | tf_op jit(solution)/shard_map/while/body/eval_jaxpr/conv_general_dilated | solution.py:29
  584.1 1.9 convolution_add_fusion.15
  586.1 2.7 copy-done.1
  589.1 0.7 add_power_fusion
  589.8 0.7 pow.19
  590.5 3.0 all-to-all-start.2
  593.8 45.9 %all-reduce.6 = (f32[]{:T(128)}, f32[8,8,4,32]{3,2,1,0:T(4,128)}, f32[32]{0:T(128)}, f32[64]{0:T(128)}, f32[64]{0:T(128)}, /*index=5*/f32[512]{0:T(512)}, f32[51...) all-reduce(f32[]{:T(128)} %get-tuple-element.432, ...), channel_id=1, replica_groups=mesh['hst'=4,'dev'=8] {'hst','dev'}, use_global_device_ids=true, to_apply=%region_12.13 | all-reduce | flops 18612 | bytes 148896 | tf_op jit(solution)/shard_map/psum | solution.py:253
  641.0 2.5 scatter_custom_fusion
  643.5 1.1 fusion.20
  644.6 40.5 %pmax.7 = f32[]{:T(128)} all-reduce(f32[]{:T(128)} %get-tuple-element.697), channel_id=1, replica_groups=mesh['hst'=4,'dev'=8] {'hst','dev'}, use_global_device_ids=true, to_apply=%region_27.28 | all-reduce | flops 1 | bytes 8 | tf_op jit(solution)/shard_map/pmax | solution.py:274
  685.1 68.2 %all-reduce.5.cloned.1.call-done = (f32[4,4,32,64]{3,2,1,0:T(8,128)}, f32[3,3,64,64]{3,2,1,0:T(8,128)}, f32[3136,512]{1,0:T(8,128)}) async-done(((f32[4,4,32,64]{3,2,1,0:T(8,128)}, f32[3,3,64,64]{3,2,1,0:T(8,128)}, f32[3136,512]{1,0:T(8,128)}), (f32[4,4,32,64]{3,2,1,0:T(8,128)}, f32[3,3,64,64]{3,2,1,0:T(8,128)}, f32[3136,512]{1,0:T(8,128)})) %all-reduce.5.cloned.1.call-update) | async-done | bytes 6701072 | tf_op jit(solution)/shard_map/psum | solution.py:253
  753.2 1.7 copy.135
  754.9 1.7 copy.136
  756.6 6.3 copy.137
  (248 shorter events, 17.5 us)
Async XLA Ops:
  8.5 64.2 %all-to-all-start.1 = ((bf16[32,1,8]{2,1,0:T(2,128)(2,1)}), bf16[32,1,8]{2,1,0:T(2,128)(2,1)S(1)}, u32[]{:S(2)}, u32[]{:S(2)}) async-start(bf16[32,1,8]{2,1,0:T(2,128)(2,1)} %compare_convert_fusion), calls=%async_computation.1 | async-start | bytes 32768 | tf_op jit(solution)/shard_map/all_to_all | solution.py:230
  17.3 10.4 %copy-start.29 = (s32[256,1]{0,1:T(1,128)}, s32[256,1]{0,1:T(1,128)S(1)}, u32[]{:S(2)}) copy-start(s32[256,1]{0,1:T(1,128)S(1)} %compare_select_fusion.2) | copy-start | bytes 3076
  72.6 6.8 copy-start.24
  72.6 6.8 copy-start.25
  72.6 7.0 copy-start.26
  72.6 7.7 %copy-start.27 = (s32[1,32,8]{1,2,0:T(8,128)S(1)}, s32[1,32,8]{1,2,0:T(8,128)}, u32[]{:S(2)}) copy-start(s32[1,32,8]{1,2,0:T(8,128)} %param.28) | copy-start | bytes 3076
  72.6 8.4 %copy-start.28 = (f32[1,32,8]{1,2,0:T(8,128)S(1)}, f32[1,32,8]{1,2,0:T(8,128)}, u32[]{:S(2)}) copy-start(f32[1,32,8]{1,2,0:T(8,128)} %param.32) | copy-start | bytes 3076
  72.7 9.1 %copy-start.33 = (bf16[18]{0:T(256)(128)(2,1)S(1)}, bf16[18]{0:T(256)(128)(2,1)}, u32[]{:S(2)}) copy-start(bf16[18]{0:T(256)(128)(2,1)} %param.45) | copy-start | bytes 112
  72.7 9.7 %copy-start.13 = (bf16[512,18]{0,1:T(8,128)(2,1)S(1)}, bf16[512,18]{0,1:T(8,128)(2,1)}, u32[]{:S(2)}) copy-start(bf16[512,18]{0,1:T(8,128)(2,1)} %param.44) | copy-start | bytes 55300
  72.7 9.7 %copy-start.30 = (bf16[512,1]{0,1:T(2,128)(2,1)S(1)}, bf16[512,1]{0,1:T(2,128)(2,1)}, u32[]{:S(2)}) copy-start(bf16[512,1]{0,1:T(2,128)(2,1)} %param.42) | copy-start | bytes 3076
  72.7 10.3 %copy-start.23 = (s32[57,18]{0,1:T(8,128)S(1)}, s32[57,18]{0,1:T(8,128)}, u32[]{:S(2)}) copy-start(s32[57,18]{0,1:T(8,128)} %param.29) | copy-start | bytes 12316
  72.7 320.9 %all-to-all-start = ((bf16[32,8,28224]{2,1,0:T(8,128)(2,1)}), bf16[32,8,28224]{2,1,0:T(8,128)(2,1)}, u32[]{:S(2)}, u32[]{:S(2)}) async-start(bf16[32,8,28224]{2,1,0:T(8,128)(2,1)} %bitcast_select_fusion), calls=%async_computation | async-start | bytes 28966912 | tf_op jit(solution)/shard_map/all_to_all | solution.py:229
  78.6 674.6 %all-reduce.5.cloned.1.call-start = ((), (), s32[]{:S(2)}) async-start(), calls=%async_computation.3 | async-start | bytes 13959168 | tf_op jit(solution)/shard_map/psum | solution.py:253
  393.6 19.8 %copy-start = (bf16[3136,512]{1,0:T(8,128)(2,1)S(1)}, bf16[3136,512]{1,0:T(8,128)(2,1)}, u32[]{:S(2)}) copy-start(bf16[3136,512]{1,0:T(8,128)(2,1)} %param.40) | copy-start | bytes 9633796
  393.6 19.8 %copy-start.12 = (bf16[512]{0:T(512)(128)(2,1)S(1)}, bf16[512]{0:T(512)(128)(2,1)}, u32[]{:S(2)}) copy-start(bf16[512]{0:T(512)(128)(2,1)} %param.41) | copy-start | bytes 3076
  434.7 26.5 %copy-start.21 = (f32[64]{0:T(128)}, f32[64]{0:T(128)S(1)}, u32[]{:S(2)}) copy-start(f32[64]{0:T(128)S(1)} %convert_element_type.222) | copy-start | bytes 772 | tf_op jit(solution)/shard_map/while
  435.4 21.5 %copy-start.36 = (f32[64]{0:T(128)}, f32[64]{0:T(128)S(1)}, u32[]{:S(2)}) copy-start(f32[64]{0:T(128)S(1)} %convert_element_type.220) | copy-start | bytes 772 | tf_op jit(solution)/shard_map/while
  436.0 7.1 copy-start.34
  456.9 4.3 copy-start.38
  461.2 3.7 copy-start.40
  477.3 7.4 slice-start.4
  478.7 3.8 copy-start.5
  478.7 3.8 copy-start.41
  478.7 5.9 slice-start.5
  482.6 13.4 %slice-start.2 = ((s8[7225344]{0:T(1024)(128)(4,1)}), s8[4194304]{0:T(1024)(128)(4,1)S(1)}, s32[]{:S(2)}) async-start(s8[7225344]{0:T(1024)(128)(4,1)} %bitcast.147), calls=%async_computation.6 | async-start | bytes 8388608 | tf_op jit(solution)/shard_map/while
  484.6 8.3 %copy-start.6 = (f32[3,3,64,64]{3,2,1,0:T(8,128)}, f32[3,3,64,64]{3,2,1,0:T(8,128)S(1)}, u32[]{:S(2)}) copy-start(f32[3,3,64,64]{3,2,1,0:T(8,128)S(1)} %convolution_add_fusion.14) | copy-start | bytes 442372 | tf_op jit(solution)/shard_map/while
  484.7 8.2 %copy-start.7 = (f32[4,4,32,64]{3,2,1,0:T(8,128)S(1)}, f32[4,4,32,64]{3,2,1,0:T(8,128)}, u32[]{:S(2)}) copy-start(f32[4,4,32,64]{3,2,1,0:T(8,128)} %get-tuple-element.1014) | copy-start | bytes 393220 | tf_op jit(solution)/shard_map/while
  484.7 8.2 %copy-start.39 = (bf16[128,20,20,32]{0,3,2,1:T(8,128)(2,1)S(1)}, bf16[128,20,20,32]{0,3,2,1:T(8,128)(2,1)}, u32[]{:S(2)}) copy-start(bf16[128,20,20,32]{0,3,2,1:T(8,128)(2,1)} %copy-done.38) | copy-start | bytes 9830404 | tf_op jit(solution)/shard_map/while
  484.7 11.2 %slice-start.3 = ((s8[7225344]{0:T(1024)(128)(4,1)}), s8[3031040]{0:T(1024)(128)(4,1)S(1)}, s32[]{:S(2)}) async-start(s8[7225344]{0:T(1024)(128)(4,1)} %bitcast.147), calls=%async_computation.7 | async-start | bytes 6062080 | tf_op jit(solution)/shard_map/while
  492.9 3.0 copy-start.9
  495.9 10.0 %copy-start.8 = (f32[4,4,32,64]{3,2,1,0:T(8,128)}, f32[4,4,32,64]{3,2,1,0:T(8,128)S(1)}, u32[]{:S(2)}) copy-start(f32[4,4,32,64]{3,2,1,0:T(8,128)S(1)} %convolution_add_fusion.13) | copy-start | bytes 393220 | tf_op jit(solution)/shard_map/while
  495.9 10.1 %slice-start = ((s8[6422528]{0:T(1024)(128)(4,1)}), s8[4194304]{0:T(1024)(128)(4,1)S(1)}, s32[]{:S(2)}) async-start(s8[6422528]{0:T(1024)(128)(4,1)} %bitcast.144), calls=%async_computation.4 | async-start | bytes 8388608 | tf_op jit(solution)/shard_map/while
  495.9 10.0 %copy-start.14 = (f32[64]{0:T(128)S(1)}, f32[64]{0:T(128)}, u32[]{:S(2)}) copy-start(f32[64]{0:T(128)} %get-tuple-element.1015) | copy-start | bytes 772 | tf_op jit(solution)/shard_map/while
  496.0 10.0 %copy-start.18 = (f32[32]{0:T(128)S(1)}, f32[32]{0:T(128)}, u32[]{:S(2)}) copy-start(f32[32]{0:T(128)} %get-tuple-element.1013) | copy-start | bytes 388 | tf_op jit(solution)/shard_map/while
  496.0 10.0 %slice-start.1 = ((s8[6422528]{0:T(1024)(128)(4,1)}), s8[2228224]{0:T(1024)(128)(4,1)S(1)}, s32[]{:S(2)}) async-start(s8[6422528]{0:T(1024)(128)(4,1)} %bitcast.144), calls=%async_computation.5 | async-start | bytes 4456448 | tf_op jit(solution)/shard_map/while
  496.0 10.0 %copy-start.3 = (bf16[128,7,7,64]{0,3,2,1:T(8,128)(2,1)S(1)}, bf16[128,7,7,64]{0,3,2,1:T(8,128)(2,1)}, u32[]{:S(2)}) copy-start(bf16[128,7,7,64]{0,3,2,1:T(8,128)(2,1)} %copy-done.2) | copy-start | bytes 2408452 | tf_op jit(solution)/shard_map/while
  512.1 26.5 %copy-start.21 = (f32[64]{0:T(128)}, f32[64]{0:T(128)S(1)}, u32[]{:S(2)}) copy-start(f32[64]{0:T(128)S(1)} %convert_element_type.222) | copy-start | bytes 772 | tf_op jit(solution)/shard_map/while
  512.8 21.5 %copy-start.36 = (f32[64]{0:T(128)}, f32[64]{0:T(128)S(1)}, u32[]{:S(2)}) copy-start(f32[64]{0:T(128)S(1)} %convert_element_type.220) | copy-start | bytes 772 | tf_op jit(solution)/shard_map/while
  513.4 7.1 copy-start.34
  534.3 4.3 copy-start.38
  538.6 3.7 copy-start.40
  555.3 7.4 slice-start.4
  556.8 3.8 copy-start.5
  556.8 3.8 copy-start.41
  556.8 5.9 slice-start.5
  560.6 13.4 %slice-start.2 = ((s8[7225344]{0:T(1024)(128)(4,1)}), s8[4194304]{0:T(1024)(128)(4,1)S(1)}, s32[]{:S(2)}) async-start(s8[7225344]{0:T(1024)(128)(4,1)} %bitcast.147), calls=%async_computation.6 | async-start | bytes 8388608 | tf_op jit(solution)/shard_map/while
  562.7 8.3 %copy-start.6 = (f32[3,3,64,64]{3,2,1,0:T(8,128)}, f32[3,3,64,64]{3,2,1,0:T(8,128)S(1)}, u32[]{:S(2)}) copy-start(f32[3,3,64,64]{3,2,1,0:T(8,128)S(1)} %convolution_add_fusion.14) | copy-start | bytes 442372 | tf_op jit(solution)/shard_map/while
  562.7 8.2 %copy-start.7 = (f32[4,4,32,64]{3,2,1,0:T(8,128)S(1)}, f32[4,4,32,64]{3,2,1,0:T(8,128)}, u32[]{:S(2)}) copy-start(f32[4,4,32,64]{3,2,1,0:T(8,128)} %get-tuple-element.1014) | copy-start | bytes 393220 | tf_op jit(solution)/shard_map/while
  562.7 8.2 %copy-start.39 = (bf16[128,20,20,32]{0,3,2,1:T(8,128)(2,1)S(1)}, bf16[128,20,20,32]{0,3,2,1:T(8,128)(2,1)}, u32[]{:S(2)}) copy-start(bf16[128,20,20,32]{0,3,2,1:T(8,128)(2,1)} %copy-done.38) | copy-start | bytes 9830404 | tf_op jit(solution)/shard_map/while
  562.8 11.2 %slice-start.3 = ((s8[7225344]{0:T(1024)(128)(4,1)}), s8[3031040]{0:T(1024)(128)(4,1)S(1)}, s32[]{:S(2)}) async-start(s8[7225344]{0:T(1024)(128)(4,1)} %bitcast.147), calls=%async_computation.7 | async-start | bytes 6062080 | tf_op jit(solution)/shard_map/while
  571.0 3.0 copy-start.9
  573.9 10.0 %copy-start.8 = (f32[4,4,32,64]{3,2,1,0:T(8,128)}, f32[4,4,32,64]{3,2,1,0:T(8,128)S(1)}, u32[]{:S(2)}) copy-start(f32[4,4,32,64]{3,2,1,0:T(8,128)S(1)} %convolution_add_fusion.13) | copy-start | bytes 393220 | tf_op jit(solution)/shard_map/while
  573.9 10.1 %slice-start = ((s8[6422528]{0:T(1024)(128)(4,1)}), s8[4194304]{0:T(1024)(128)(4,1)S(1)}, s32[]{:S(2)}) async-start(s8[6422528]{0:T(1024)(128)(4,1)} %bitcast.144), calls=%async_computation.4 | async-start | bytes 8388608 | tf_op jit(solution)/shard_map/while
  574.0 10.0 %copy-start.14 = (f32[64]{0:T(128)S(1)}, f32[64]{0:T(128)}, u32[]{:S(2)}) copy-start(f32[64]{0:T(128)} %get-tuple-element.1015) | copy-start | bytes 772 | tf_op jit(solution)/shard_map/while
  574.0 10.0 %copy-start.18 = (f32[32]{0:T(128)S(1)}, f32[32]{0:T(128)}, u32[]{:S(2)}) copy-start(f32[32]{0:T(128)} %get-tuple-element.1013) | copy-start | bytes 388 | tf_op jit(solution)/shard_map/while
  574.0 10.0 %slice-start.1 = ((s8[6422528]{0:T(1024)(128)(4,1)}), s8[2228224]{0:T(1024)(128)(4,1)S(1)}, s32[]{:S(2)}) async-start(s8[6422528]{0:T(1024)(128)(4,1)} %bitcast.144), calls=%async_computation.5 | async-start | bytes 4456448 | tf_op jit(solution)/shard_map/while
  574.0 10.0 %copy-start.3 = (bf16[128,7,7,64]{0,3,2,1:T(8,128)(2,1)S(1)}, bf16[128,7,7,64]{0,3,2,1:T(8,128)(2,1)}, u32[]{:S(2)}) copy-start(bf16[128,7,7,64]{0,3,2,1:T(8,128)(2,1)} %copy-done.2) | copy-start | bytes 2408452 | tf_op jit(solution)/shard_map/while
  589.0 4.6 copy-start.31
  589.0 4.7 copy-start.11
  589.0 4.7 copy-start.16
  589.0 4.7 copy-start.17
  589.0 4.7 copy-start.20
  589.1 54.4 %copy-start.32 = (f32[128]{0:T(128)S(1)}, f32[128]{0:T(128)}, u32[]{:S(2)}) copy-start(f32[128]{0:T(128)} %param.33) | copy-start | bytes 1540
  590.5 49.2 %all-to-all-start.2 = ((f32[32,1,8]{2,1,0:T(1,128)}), f32[32,1,8]{2,1,0:T(1,128)S(1)}, u32[]{:S(2)}, u32[]{:S(2)}) async-start(f32[32,1,8]{2,1,0:T(1,128)} %bitcast.6), calls=%async_computation.2 | async-start | bytes 32768 | tf_op jit(solution)/shard_map/all_to_all | solution.py:246
  (20 other events, 35.9 us)
Sparse Core Ops, SparseCore 0:
  589.2 163.9 all-reduce.4
where the time goes:
time: 782 us; the launch traced here: 770 us
  waiting for transfers between devices  377 us (48%)
  matrix products  112 us (14%)
  local copies, waits for them, and re-layouts  107 us (14%)
  blocking collectives  86.4 us (11%)
  other arithmetic  33.1 us (4%)
  loops' own time  22.4 us (3%)
  starting transfers between devices  16 us (2%)
  between operations  15.4 us (2%)
    all_to_all x1, waiting for transfers between devices, per_device(): lax.all_to_all(packed, ('hst', 'dev'), split_axis=0, concat_axis=0, tiled...  309 us
    psum x1, waiting for transfers between devices, per_device(): lax.psum((loss_local, grads[0], grads[1], grads[2], grads[3], grads[4], g...  68.2 us
    psum x1, blocking collectives, per_device(): lax.psum((loss_local, grads[0], grads[1], grads[2], grads[3], grads[4], g...  45.9 us
    conv_general_dilated x6, matrix products, forward_conv(): lax.conv_general_dilated(source, kernel, (stride, stride), 'VALID', dimen...  43.6 us
    unnamed x45, local copies, waits for them, and re-layouts  40.9 us
    pmax x1, blocking collectives, per_device(): top_priority = lax.pmax(jnp.max(new_table), ('hst', 'dev'))  40.5 us
    gather x1, local copies, waits for them, and re-layouts, per_device(): jnp.take(replay, own_index.reshape(-1), axis=0)  31.6 us
    conv_general_dilated x6, matrix products, kernel_grad(): lax.conv_general_dilated(source, upstream, (1, 1), 'VALID', rhs_dilation=...  29.8 us
  transfers between devices with their start and end apart: 4, of which 2 were waited for; matrix products, arithmetic and copies ran while one was open for 9% of the time, Pallas kernels for 0%

commit v1 on v0

v1 whole, which is shorter than its diff:
```python
import jax
import jax.numpy as jnp
from jax import lax
from jax.sharding import PartitionSpec as P

FRAME = 84
STACK = 4
S1 = 4
S2 = 2
S3 = 1


GAMMA_THREE = 0.970299
PLAIN_SPEC = ("NHWC", "HWIO", "NHWC")


def forward_conv(source, kernel, stride):
    return lax.conv_general_dilated(
        source,
        kernel,
        (stride, stride),
        "VALID",
        dimension_numbers=PLAIN_SPEC,
        preferred_element_type=jnp.float32,
    )


def kernel_grad(source, upstream, stride):
    return lax.conv_general_dilated(
        source,
        upstream,
        (1, 1),
        "VALID",
        rhs_dilation=(stride, stride),
        dimension_numbers=("CHWN", "IHWO", "HWNC"),
        preferred_element_type=jnp.float32,
    )


def source_grad(upstream, kernel, stride):
    margin = kernel.shape[0] - 1
    return lax.conv_general_dilated(
        upstream,
        jnp.flip(kernel, (0, 1)),
        (1, 1),
        ((margin, margin), (margin, margin)),
        lhs_dilation=(stride, stride),
        dimension_numbers=("NHWC", "HWOI", "NHWC"),
        preferred_element_type=jnp.float32,
    )


def silu_slope(pre_value):
    gate_value = jax.nn.sigmoid(pre_value)
    return gate_value * (1.0 + pre_value * (1.0 - gate_value))


def huber(td_error):
    magnitude = jnp.abs(td_error)
    return jnp.where(magnitude <= 1.0, 0.5 * td_error * td_error, magnitude - 0.5)


def transposed_dot(left_side, right_side):
    return lax.dot_general(
        left_side, right_side, (((0,), (0,)), ((), ())), preferred_element_type=jnp.float32
    )


def learn(pictures, meta, own_index, own_live, legal_table, params):
    (
        conv1_w,
        conv1_b,
        conv2_w,
        conv2_b,
        conv3_w,
        conv3_b,
        dense_w,
        dense_b,
        value_w,
        value_b,
        advantage_w,
        advantage_b,
    ) = params
    row_count = pictures.shape[0]
    slot_count = own_index.shape[0]
    action_rows, game_rows, target_rows, weight_rows = meta
    head_w = jnp.concatenate([value_w, advantage_w], 1)
    head_b = jnp.concatenate([value_b, advantage_b], 0).astype(jnp.float32)
    game_count = legal_table.shape[0]
    action_count = legal_table.shape[1]
    noop_mask = (jnp.arange(action_count) == 0).astype(jnp.float32)
    legal_rows = jnp.maximum(legal_table.astype(jnp.float32), noop_mask[None, :])
    row_pick = (own_index[:, None] == jnp.arange(row_count)[None, :]).astype(jnp.float32)

    pre_one = forward_conv(pictures, conv1_w, S1) + conv1_b.astype(jnp.float32)
    act_one = jax.nn.silu(pre_one).astype(jnp.bfloat16)
    pre_two = forward_conv(act_one, conv2_w, S2) + conv2_b.astype(jnp.float32)
    act_two = jax.nn.silu(pre_two).astype(jnp.bfloat16)
    pre_three = forward_conv(act_two, conv3_w, S3) + conv3_b.astype(jnp.float32)
    act_three = jax.nn.silu(pre_three).astype(jnp.bfloat16)
    flat_three = act_three.reshape(row_count, -1)
    pre_dense = jnp.dot(
        flat_three, dense_w, preferred_element_type=jnp.float32
    ) + dense_b.astype(jnp.float32)
    act_dense = jax.nn.silu(pre_dense).astype(jnp.bfloat16)
    head_rows = jnp.dot(act_dense, head_w, preferred_element_type=jnp.float32) + head_b
    head_out = jnp.dot(row_pick, head_rows, precision=lax.Precision.HIGHEST)
    state_value = head_out[:, :1]
    advantage = head_out[:, 1:]
    game_pick = (game_rows[:, None] == jnp.arange(game_count)[None, :]).astype(jnp.float32)
    legal_mask = jnp.dot(game_pick, legal_rows, precision=lax.Precision.HIGHEST)
    counted = jnp.sum(legal_mask, 1)
    centre = jnp.sum(advantage * legal_mask, 1) / counted
    q_part = state_value + advantage - centre[:, None]
    act_pick = (action_rows[:, None] == jnp.arange(action_count)[None, :]).astype(jnp.float32)
    td_error = target_rows - jnp.sum(q_part * act_pick, 1)
    scaled = own_live * weight_rows
    loss = jnp.sum(scaled * huber(td_error)) / slot_count
    grad_taken = -scaled * jnp.clip(td_error, -1.0, 1.0) / slot_count
    grad_q = grad_taken[:, None] * act_pick
    grad_value = jnp.sum(grad_q, 1, keepdims=True)
    grad_adv = grad_q - legal_mask * (jnp.sum(grad_q, 1) / counted)[:, None]
    grad_head = jnp.concatenate([grad_value, grad_adv], 1).astype(jnp.bfloat16).astype(jnp.float32)
    grad_head = lax.dot_general(
        row_pick, grad_head, (((0,), (0,)), ((), ())), precision=lax.Precision.HIGHEST
    )
    head_w_grad = lax.dot_general(
        act_dense.astype(jnp.float32), grad_head, (((0,), (0,)), ((), ())), precision=lax.Precision.HIGHEST
    )
    head_b_grad = jnp.sum(grad_head, 0)
    up_dense = lax.dot_general(
        grad_head, head_w.astype(jnp.float32), (((1,), (1,)), ((), ())), precision=lax.Precision.HIGHEST
    )
    grad_dense = (up_dense * silu_slope(pre_dense)).astype(jnp.bfloat16)
    dense_w_grad = transposed_dot(flat_three, grad_dense)
    dense_b_grad = jnp.sum(grad_dense.astype(jnp.float32), 0)
    up_three = lax.dot_general(
        grad_dense, dense_w, (((1,), (1,)), ((), ())), preferred_element_type=jnp.float32
    ).reshape(act_three.shape)
    grad_three = (up_three * silu_slope(pre_three)).astype(jnp.bfloat16)
    conv3_w_grad = kernel_grad(act_two, grad_three, S3)
    conv3_b_grad = jnp.sum(grad_three.astype(jnp.float32), (0, 1, 2))
    up_two = source_grad(grad_three, conv3_w, S3)
    grad_two = (up_two * silu_slope(pre_two)).astype(jnp.bfloat16)
    conv2_w_grad = kernel_grad(act_one, grad_two, S2)
    conv2_b_grad = jnp.sum(grad_two.astype(jnp.float32), (0, 1, 2))
    up_one = source_grad(grad_two, conv2_w, S2)
    grad_one = (up_one * silu_slope(pre_one)).astype(jnp.bfloat16)
    conv1_w_grad = kernel_grad(pictures, grad_one, S1)
    conv1_b_grad = jnp.sum(grad_one.astype(jnp.float32), (0, 1, 2))
    grads = (
        conv1_w_grad,
        conv1_b_grad,
        conv2_w_grad,
        conv2_b_grad,
        conv3_w_grad,
        conv3_b_grad,
        dense_w_grad,
        dense_b_grad,
        head_w_grad[:, :1],
        head_b_grad[:1],
        head_w_grad[:, 1:],
        head_b_grad[1:],
    )
    return q_part, td_error, loss, grads


def per_device(
    replay,
    send_index,
    send_count,
    actions,
    game_ids,
    legal_table,
    returns,
    bootstrap,
    is_weights,
    priority_table,
    *params,
):
    axes = ("hst", "dev")
    peer_count = send_index.shape[1]
    capacity = send_index.shape[2]
    own_index = send_index[0].reshape(-1)
    own_live = (
        jnp.arange(capacity, dtype=jnp.int32)[None, :] < send_count[0][:, None]
    ).astype(jnp.float32).reshape(-1)
    targets = returns[0] + GAMMA_THREE * bootstrap[0]
    outgoing = jnp.stack(
        [actions[0].astype(jnp.float32), game_ids[0].astype(jnp.float32), targets, is_weights[0]], 1
    )
    meta = lax.all_to_all(outgoing, axes, split_axis=0, concat_axis=0, tiled=True)
    meta = (
        meta[:, 0].reshape(-1).astype(jnp.int32),
        meta[:, 1].reshape(-1).astype(jnp.int32),
        meta[:, 2].reshape(-1),
        meta[:, 3].reshape(-1),
    )
    pictures = replay.reshape(replay.shape[0], FRAME, FRAME, STACK)
    q_part, td_rows, loss_local, grads = learn(
        pictures, meta, own_index, own_live, legal_table, params
    )
    q_values = lax.all_to_all(
        q_part.reshape(peer_count, capacity, -1), axes, split_axis=0, concat_axis=0, tiled=True
    ).reshape(1, peer_count * capacity, -1)
    totals = lax.psum((loss_local,) + grads, axes)
    candidates = own_live * ((td_rows * td_rows + 1.0) ** 0.3)
    fresh = jnp.max(
        jnp.where(own_index[:, None] == jnp.arange(replay.shape[0])[None, :], candidates[:, None], 0.0), 0
    )
    new_table = jnp.where(fresh > 0.0, fresh, priority_table)
    top_priority = lax.pmax(jnp.max(new_table), axes)
    return (q_values,) + totals + (new_table, top_priority)


def solution(mesh):
    placed = (
        P(("hst", "dev"), None),
        P(("hst", "dev"), None, None),
        P(("hst", "dev"), None),
        P(("hst", "dev"), None, None),
        P(("hst", "dev"), None, None),
        P(),
        P(("hst", "dev"), None, None),
        P(("hst", "dev"), None, None),
        P(("hst", "dev"), None, None),
        P(("hst", "dev")),
        P(),
        P(),
        P(),
        P(),
        P(),
        P(),
        P(),
        P(),
        P(),
        P(),
        P(),
        P(),
    )
    return jax.shard_map(
        per_device,
        mesh=mesh,
        in_specs=placed,
        out_specs=(
            P(("hst", "dev"), None, None),
            P(),
            P(),
            P(),
            P(),
            P(),
            P(),
            P(),
            P(),
            P(),
            P(),
            P(),
            P(),
            P(),
            P(("hst", "dev")),
            P(),
        ),
        check_vma=False,
    )
```

time: 782 us -> 267 us (0.34); the launches traced: 770 us -> 265 us
  waiting for transfers between devices: 377 us -> 55.7 us
  local copies, waits for them, and re-layouts: 107 us -> 19 us
  matrix products: 112 us -> 62.4 us
  loops' own time: 22.4 us -> 0 us
  other arithmetic: 33.1 us -> 16.2 us
    all_to_all x3 -> x2, waiting for transfers between devices: 309 us -> 0.01 us  [the longest x1 0.01 us: per_device(): lax.all_to_all(outgoing, axes, split_axis=0, concat_axis=0, tiled=True)]
    gather x1 -> x0, local copies, waits for them, and re-layouts: 31.6 us -> none  [per_device(): jnp.take(replay, own_index.reshape(-1), axis=0)]
    unnamed x45 -> x71, local copies, waits for them, and re-layouts: 40.9 us -> 14.7 us
    conv_general_dilated x6 -> x3, matrix products: 43.6 us -> 19.8 us  [forward_conv(): lax.conv_general_dilated(source, kernel, (stride, stride), 'VALID', dimen...]
    another operation x1 -> x0, loops' own time: 22.4 us -> none  [learn(): lax.scan(one_block, (starting, jnp.zeros((), jnp.float32)), pieces)]
    select_n x3 -> x0, other arithmetic: 13.4 us -> none  [the longest x2 13.4 us: per_device(): jnp.take(replay, own_index.reshape(-1), axis=0)]
    dynamic_slice x2 -> x0, local copies, waits for them, and re-layouts: 12.9 us -> none  [learn(): lax.scan(one_block, (starting, jnp.zeros((), jnp.float32)), pieces)]
    psum x1, waiting for transfers between devices: 68.2 us -> 55.6 us  [per_device(): totals = lax.psum((loss_local,) + grads, axes)]
  transfers between devices with their start and end apart: 4 -> 3, of which waited for: 2 -> 1; matrix products, arithmetic and copies ran while one was open for 9% -> 25% of each run, Pallas kernels for 0% -> 0%
where the time goes in v1:
time: 267 us; the launch traced here: 265 us
  blocking collectives  83.4 us (31%)
  matrix products  62.4 us (23%)
  waiting for transfers between devices  55.7 us (21%)
  local copies, waits for them, and re-layouts  19 us (7%)
  other arithmetic  16.2 us (6%)
  between operations  15.7 us (6%)
  starting transfers between devices  13 us (5%)
    psum x1, waiting for transfers between devices, per_device(): totals = lax.psum((loss_local,) + grads, axes)  55.6 us
    psum x1, blocking collectives, per_device(): totals = lax.psum((loss_local,) + grads, axes)  43.2 us
    pmax x1, blocking collectives, per_device(): top_priority = lax.pmax(jnp.max(new_table), axes)  40.2 us
    conv_general_dilated x3, matrix products, forward_conv(): lax.conv_general_dilated(source, kernel, (stride, stride), 'VALID', dimen...  19.8 us
    conv_general_dilated x3, matrix products, kernel_grad(): lax.conv_general_dilated(source, upstream, (1, 1), 'VALID', rhs_dilation=...  18.3 us
    unnamed x71, local copies, waits for them, and re-layouts  14.7 us
    conv_general_dilated x2, matrix products, source_grad(): lax.conv_general_dilated(upstream, jnp.flip(kernel, (0, 1)), (1, 1), ((ma...  12.7 us
    all_to_all x1, starting transfers between devices, per_device(): lax.all_to_all(outgoing, axes, split_axis=0, concat_axis=0, tiled=True)  7.1 us
  transfers between devices with their start and end apart: 3, of which 1 were waited for; matrix products, arithmetic and copies ran while one was open for 25% of the time, Pallas kernels for 0%

profile of v1, /device:TPU:1, one launch (start us, length us, event | category | flops | bytes accessed | tf_op | source)
XLA Modules:
  0.0 265.4 jit_solution(2459578493739955173)
XLA Ops:
  7.2 0.9 add_bitcast_fusion
  8.1 0.8 convert_bitcast_fusion
  8.9 0.7 pad_maximum_fusion.1
  9.6 0.7 copy.53
  10.3 7.1 %all-to-all-start = ((f32[32,4,8]{2,1,0:T(4,128)}), f32[32,4,8]{2,1,0:T(4,128)S(1)}, u32[]{:S(2)}, u32[]{:S(2)}) async-start(f32[32,4,8]{2,1,0:T(4,128)} %copy.53), calls=%async_computation | async-start | bytes 131072 | tf_op jit(solution)/shard_map/all_to_all | solution.py:192
  18.1 0.7 convert_element_type.123
  18.7 0.7 convert_element_type.125
  19.4 0.7 convert_element_type.127
  20.0 0.7 convert_element_type.129
  20.7 0.7 iota_compare_fusion.6
  21.4 0.8 copy.52
  22.2 0.1 eq.26
  22.3 0.7 maximum_convert_fusion
  23.0 13.8 %multiply_convert_fusion.1 = (bf16[128,20,20,32]{0,3,2,1:T(8,128)(2,1)S(1)}, f32[128,20,20,32]{0,3,2,1:T(8,128)}) fusion(f32[32]{0:T(128)S(1)} %convert_element_type.123, bf16[128,84,84,4]{0,3,2,1:T(4,128)(2,1)} %bitcast.62, bf16[8,8,4,32]{3,2,1,0:T(4,128)(2,1)} %param.32), kind=kOutput, calls=%fused_computation.2 | convolution fusion | flops 848691200 | bytes 17072256 | tf_op jit(solution)/shard_map/conv_general_dilated | solution.py:18
  36.9 3.3 %multiply_convert_fusion.3 = (bf16[128,9,9,64]{0,3,2,1:T(8,128)(2,1)S(1)}, f32[128,9,9,64]{0,3,2,1:T(8,128)}) fusion(f32[64]{0:T(128)S(1)} %convert_element_type.125, bf16[128,20,20,32]{0,3,2,1:T(8,128)(2,1)S(1)} %get-tuple-element.93, bf16[4,4,32,64]{3,2,1,0:T(8,128)(2,1)S(1)} %copy-done.20), kind=kOutput, calls=%fused_computation.6 | convolution fusion | flops 683458560 | bytes 7323904 | tf_op jit(solution)/shard_map/conv_general_dilated | solution.py:18
  40.2 2.7 %multiply_convert_fusion.5 = (bf16[128,7,7,64]{0,3,2,1:T(8,128)(2,1)S(1)}, f32[128,7,7,64]{0,3,2,1:T(8,128)}) fusion(f32[64]{0:T(128)S(1)} %convert_element_type.127, bf16[128,9,9,64]{0,3,2,1:T(8,128)(2,1)S(1)} %get-tuple-element.95, bf16[3,3,64,64]{3,2,1,0:T(8,128)(2,1)S(1)} %copy-done.18), kind=kOutput, calls=%fused_computation.10 | convolution fusion | flops 464830464 | bytes 3809536 | tf_op jit(solution)/shard_map/conv_general_dilated | solution.py:18
  42.9 0.9 copy-done.1
  43.8 1.4 multiply_convert_fusion.6
  45.1 0.1 convolution_add_fusion.1
  45.3 0.3 fusion.2
  45.6 0.6 lt.46
  46.2 0.6 slice.40
  46.7 0.1 fusion.11
  46.9 0.7 convert_element_type.141
  47.5 0.1 reshape_squeeze.8
  47.6 0.1 reshape_squeeze.9
  47.7 0.1 convert_element_type.137
  47.8 0.3 fusion.22
  48.1 0.7 select_reduce_fusion.2
  48.8 0.7 reduce_sum.99
  49.5 0.7 power_select_fusion
  50.2 0.7 select_reduce_fusion.1
  50.9 0.7 fusion.7
  51.6 1.5 fusion.26
  53.1 1.9 convert_reduce_fusion.3
  55.0 2.2 fusion.30
  57.2 3.9 %fusion.31 = f32[3136,512]{1,0:T(8,128)} fusion(bf16[128,3136]{0,1:T(8,128)(2,1)S(1)} %bitcast.50, bf16[128,512]{1,0:T(8,128)(2,1)S(1)} %get-tuple-element.107), kind=kOutput, calls=%fused_computation.73 | convolution fusion | flops 411041792 | bytes 7356416 | tf_op jit(solution)/shard_map/dot_general | solution.py:64
  61.1 0.1 select_reduce_fusion
  61.2 0.1 copy.54
  61.4 0.8 reshape.238
  62.1 5.9 %all-to-all-start.1 = ((f32[32,1,144]{2,1,0:T(1,128)}), f32[32,1,144]{2,1,0:T(1,128)}, u32[]{:S(2)}, u32[]{:S(2)}) async-start(f32[32,1,144]{2,1,0:T(1,128)} %reshape.238), calls=%async_computation.1 | async-start | bytes 65536 | tf_op jit(solution)/shard_map/all_to_all | solution.py:203
  68.0 0.0 all-reduce.5.cloned.1.call-start
  68.1 3.3 %convert_reduce_fusion.2 = (f32[64]{0:T(128)}, bf16[128,7,7,64]{0,3,2,1:T(8,128)(2,1)S(1)}) fusion(f32[128,7,7,64]{0,3,2,1:T(8,128)} %bitcast.48, f32[128,7,7,64]{0,3,2,1:T(8,128)} %get-tuple-element.98, f32[64]{0:T(128)S(1)} %copy-done.14), kind=kLoop, calls=%fused_computation.8 | loop fusion | flops 4816832 | bytes 4014592 | tf_op jit(solution)/shard_map/reduce_sum | solution.py:142
  71.4 2.7 %fusion.29 = f32[3,3,64,64]{3,2,1,0:T(8,128)} fusion(bf16[128,9,9,64]{0,3,2,1:T(8,128)(2,1)S(1)} %copy-done.30, bf16[128,7,7,64]{0,3,2,1:T(8,128)(2,1)S(1)} %get-tuple-element.84), kind=kOutput, calls=%fused_computation.71 | convolution fusion | flops 462422016 | bytes 2277376 | tf_op jit(solution)/shard_map/conv_general_dilated | solution.py:29
  74.2 3.2 %convert_reduce_fusion.1 = (f32[64]{0:T(128)}, bf16[128,9,9,64]{0,3,2,1:T(8,128)(2,1)S(1)}) fusion(f32[128,9,9,64]{0,3,2,1:T(8,128)S(1)} %copy-done.31, f32[64]{0:T(128)S(1)} %copy-done.25, bf16[128,7,7,64]{0,3,2,1:T(8,128)(2,1)S(1)} %get-tuple-element.84, bf16[3,3,64,64]{3,2,1,0:T(8,128)(2,1)S(1)} %copy-done.19), kind=kOutput, calls=%fused_computation.4 | convolution fusion | flops 470384576 | bytes 4858368 | tf_op jit(solution)/shard_map/conv_general_dilated | solution.py:42
  77.4 1.1 copy-done.28
  78.5 3.6 %fusion.28 = f32[4,4,32,64]{3,2,1,0:T(8,128)} fusion(bf16[128,20,20,32]{0,3,2,1:T(8,128)(2,1)S(1)} %copy-done.27, bf16[128,9,9,64]{0,3,2,1:T(8,128)(2,1)S(1)} %get-tuple-element.105), kind=kOutput, calls=%fused_computation.70 | convolution fusion | flops 679477248 | bytes 4734976 | tf_op jit(solution)/shard_map/conv_general_dilated | solution.py:29
  82.1 0.6 copy-done.17
  82.7 1.1 fusion.23
  83.8 0.2 fusion.32
  84.0 9.4 %convert_reduce_fusion = (f32[32]{0:T(128)S(1)}, bf16[128,20,20,32]{0,3,2,1:T(8,128)(2,1)S(1)}) fusion(f32[128,20,20,32]{0,3,2,1:T(8,128)} %get-tuple-element.94, f32[32]{0:T(128)S(1)} %copy-done.23, bf16[128,9,9,64]{0,3,2,1:T(8,128)(2,1)} %copy-done.28, bf16[4,4,32,64]{3,2,1,0:T(8,128)(2,1)} %param.34), kind=kOutput, calls=%fused_computation | convolution fusion | flops 699138048 | bytes 11223296 | tf_op jit(solution)/shard_map/conv_general_dilated | solution.py:42
  93.5 12.0 %fusion.27 = f32[8,8,4,32]{3,2,1,0:T(4,128)S(1)} fusion(bf16[128,84,84,4]{0,3,2,1:T(4,128)(2,1)} %bitcast.63, bf16[128,20,20,32]{0,3,2,1:T(8,128)(2,1)S(1)} %get-tuple-element.103), kind=kOutput, calls=%fused_computation.69 | convolution fusion | flops 838860800 | bytes 10534912 | tf_op jit(solution)/shard_map/conv_general_dilated | solution.py:29
  105.6 0.7 fusion.10
  106.3 40.2 %pmax.7 = f32[]{:T(128)} all-reduce(f32[]{:T(128)} %get-tuple-element.81), channel_id=1, replica_groups=mesh['hst'=4,'dev'=8] {'hst','dev'}, use_global_device_ids=true, to_apply=%region_25.26 | all-reduce | flops 1 | bytes 8 | tf_op jit(solution)/shard_map/pmax | solution.py:212
  146.5 0.1 slice.39
  147.2 43.2 %all-reduce.6 = (f32[]{:T(128)}, f32[8,8,4,32]{3,2,1,0:T(4,128)}, f32[32]{0:T(128)}, f32[64]{0:T(128)}, f32[64]{0:T(128)}, /*index=5*/f32[512]{0:T(512)}, f32[51...) all-reduce(f32[]{:T(128)S(6)} %div.48, ...), channel_id=1, replica_groups=mesh['hst'=4,'dev'=8] {'hst','dev'}, use_global_device_ids=true, to_apply=%region_4.5 | all-reduce | flops 18612 | bytes 148896 | tf_op jit(solution)/shard_map/psum | solution.py:206
  190.5 0.5 broadcast.128
  191.0 1.5 reduce.9
  192.5 0.1 reshape.239
  192.6 0.7 copy.57
  193.3 55.6 %all-reduce.5.cloned.1.call-done = (f32[4,4,32,64]{3,2,1,0:T(8,128)}, f32[3,3,64,64]{3,2,1,0:T(8,128)}, f32[3136,512]{1,0:T(8,128)}) async-done(((f32[4,4,32,64]{3,2,1,0:T(8,128)}, f32[3,3,64,64]{3,2,1,0:T(8,128)}, f32[3136,512]{1,0:T(8,128)}), (f32[4,4,32,64]{3,2,1,0:T(8,128)}, f32[3,3,64,64]{3,2,1,0:T(8,128)}, f32[3136,512]{1,0:T(8,128)})) %all-reduce.5.cloned.1.call-update) | async-done | bytes 6701072 | tf_op jit(solution)/shard_map/psum | solution.py:206
  248.9 1.7 copy.74
  250.6 1.7 copy.75
  252.3 6.3 %copy.76 = f32[3136,512]{1,0:T(8,128)} copy(f32[3136,512]{1,0:T(8,128)} %get-tuple-element.120) | data formatting | bytes 12845056
  (71 shorter events, 0.2 us)
Async XLA Ops:
  7.2 36.6 %copy-start = (bf16[3136,512]{1,0:T(8,128)(2,1)S(1)}, bf16[3136,512]{1,0:T(8,128)(2,1)}, u32[]{:S(2)}) copy-start(bf16[3136,512]{1,0:T(8,128)(2,1)} %param.38) | copy-start | bytes 9633796
  10.3 36.4 %all-to-all-start = ((f32[32,4,8]{2,1,0:T(4,128)}), f32[32,4,8]{2,1,0:T(4,128)S(1)}, u32[]{:S(2)}, u32[]{:S(2)}) async-start(f32[32,4,8]{2,1,0:T(4,128)} %copy.53), calls=%async_computation | async-start | bytes 131072 | tf_op jit(solution)/shard_map/all_to_all | solution.py:192
  18.7 18.1 %copy-start.22 = (f32[32]{0:T(128)}, f32[32]{0:T(128)S(1)}, u32[]{:S(2)}) copy-start(f32[32]{0:T(128)S(1)} %convert_element_type.123) | copy-start | bytes 388
  19.4 17.5 %copy-start.24 = (f32[64]{0:T(128)}, f32[64]{0:T(128)S(1)}, u32[]{:S(2)}) copy-start(f32[64]{0:T(128)S(1)} %convert_element_type.125) | copy-start | bytes 772
  20.0 20.1 %copy-start.13 = (f32[64]{0:T(128)}, f32[64]{0:T(128)S(1)}, u32[]{:S(2)}) copy-start(f32[64]{0:T(128)S(1)} %convert_element_type.127) | copy-start | bytes 772
  22.3 23.0 %copy-start.7 = (s32[256]{0:T(256)}, s32[256]{0:T(256)S(1)}, u32[]{:S(2)}) copy-start(s32[256]{0:T(256)S(1)} %eq.26) | copy-start | bytes 3076
  23.0 13.8 %copy-start.20 = (bf16[4,4,32,64]{3,2,1,0:T(8,128)(2,1)S(1)}, bf16[4,4,32,64]{3,2,1,0:T(8,128)(2,1)}, u32[]{:S(2)}) copy-start(bf16[4,4,32,64]{3,2,1,0:T(8,128)(2,1)} %param.34) | copy-start | bytes 196612
  36.8 3.3 %copy-start.26 = (bf16[128,20,20,32]{0,3,2,1:T(8,128)(2,1)}, bf16[128,20,20,32]{0,3,2,1:T(8,128)(2,1)S(1)}, u32[]{:S(2)}) copy-start(bf16[128,20,20,32]{0,3,2,1:T(8,128)(2,1)S(1)} %get-tuple-element.93) | copy-start | bytes 9830404
  36.8 3.3 %copy-start.18 = (bf16[3,3,64,64]{3,2,1,0:T(8,128)(2,1)S(1)}, bf16[3,3,64,64]{3,2,1,0:T(8,128)(2,1)}, u32[]{:S(2)}) copy-start(bf16[3,3,64,64]{3,2,1,0:T(8,128)(2,1)} %param.36) | copy-start | bytes 221188
  40.2 2.7 %copy-start.29 = (bf16[128,9,9,64]{0,3,2,1:T(8,128)(2,1)}, bf16[128,9,9,64]{0,3,2,1:T(8,128)(2,1)S(1)}, u32[]{:S(2)}) copy-start(bf16[128,9,9,64]{0,3,2,1:T(8,128)(2,1)S(1)} %get-tuple-element.95) | copy-start | bytes 3981316
  42.9 0.9 copy-start.1
  42.9 2.2 copy-start.4
  42.9 2.2 copy-start.9
  42.9 4.9 %copy-start.21 = (s32[57,18]{0,1:T(8,128)S(1)}, s32[57,18]{0,1:T(8,128)}, u32[]{:S(2)}) copy-start(s32[57,18]{0,1:T(8,128)} %param.27) | copy-start | bytes 12316
  53.1 4.1 %copy-start.5 = (f32[128,19]{0,1:T(8,128)}, f32[128,19]{0,1:T(8,128)S(1)}, u32[]{:S(2)}) copy-start(f32[128,19]{0,1:T(8,128)S(1)} %get-tuple-element.109) | copy-start | bytes 29188
  55.0 2.2 copy-start.2
  57.2 3.9 %copy-start.8 = (s32[256]{0:T(256)S(1)}, s32[256]{0:T(256)}, u32[]{:S(2)}) copy-start(s32[256]{0:T(256)} %copy-done.7) | copy-start | bytes 3076
  57.2 10.9 %copy-start.14 = (f32[64]{0:T(128)S(1)}, f32[64]{0:T(128)}, u32[]{:S(2)}) copy-start(f32[64]{0:T(128)} %copy-done.13) | copy-start | bytes 772
  62.1 128.4 %all-to-all-start.1 = ((f32[32,1,144]{2,1,0:T(1,128)}), f32[32,1,144]{2,1,0:T(1,128)}, u32[]{:S(2)}, u32[]{:S(2)}) async-start(f32[32,1,144]{2,1,0:T(1,128)} %reshape.238), calls=%async_computation.1 | async-start | bytes 65536 | tf_op jit(solution)/shard_map/all_to_all | solution.py:203
  68.0 180.9 %all-reduce.5.cloned.1.call-start = ((), (), s32[]{:S(2)}) async-start(), calls=%async_computation.2 | async-start | bytes 13959168 | tf_op jit(solution)/shard_map/psum | solution.py:206
  68.1 3.4 %copy-start.30 = (bf16[128,9,9,64]{0,3,2,1:T(8,128)(2,1)S(1)}, bf16[128,9,9,64]{0,3,2,1:T(8,128)(2,1)}, u32[]{:S(2)}) copy-start(bf16[128,9,9,64]{0,3,2,1:T(8,128)(2,1)} %copy-done.29) | copy-start | bytes 3981316
  71.4 2.7 %copy-start.19 = (bf16[3,3,64,64]{3,2,1,0:T(8,128)(2,1)S(1)}, bf16[3,3,64,64]{3,2,1,0:T(8,128)(2,1)}, u32[]{:S(2)}) copy-start(bf16[3,3,64,64]{3,2,1,0:T(8,128)(2,1)} %param.36) | copy-start | bytes 221188
  71.4 2.7 %copy-start.25 = (f32[64]{0:T(128)S(1)}, f32[64]{0:T(128)}, u32[]{:S(2)}) copy-start(f32[64]{0:T(128)} %copy-done.24) | copy-start | bytes 772
  71.4 2.7 %copy-start.31 = (f32[128,9,9,64]{0,3,2,1:T(8,128)S(1)}, f32[128,9,9,64]{0,3,2,1:T(8,128)}, u32[]{:S(2)}) copy-start(f32[128,9,9,64]{0,3,2,1:T(8,128)} %get-tuple-element.96) | copy-start | bytes 7962628
  74.2 4.3 %copy-start.27 = (bf16[128,20,20,32]{0,3,2,1:T(8,128)(2,1)S(1)}, bf16[128,20,20,32]{0,3,2,1:T(8,128)(2,1)}, u32[]{:S(2)}) copy-start(bf16[128,20,20,32]{0,3,2,1:T(8,128)(2,1)} %copy-done.26) | copy-start | bytes 9830404
  77.4 1.1 copy-start.28
  82.1 0.7 copy-start.17
  82.1 1.8 copy-start.6
  82.1 1.9 copy-start.23
  93.5 12.1 %copy-start.3 = (f32[32,1,8]{2,0,1:T(8,128)S(1)}, f32[32,1,8]{2,0,1:T(8,128)}, u32[]{:S(2)}) copy-start(f32[32,1,8]{2,0,1:T(8,128)} %reduce_sum.99) | copy-start | bytes 3076
  93.5 12.1 %copy-start.12 = (s32[1,32]{1,0:T(1,128)S(1)}, s32[1,32]{1,0:T(1,128)}, u32[]{:S(2)}) copy-start(s32[1,32]{1,0:T(1,128)} %param.24) | copy-start | bytes 388
  93.5 53.0 %copy-start.15 = (f32[19]{0:T(128)S(1)}, f32[19]{0:T(128)}, u32[]{:S(2)}) copy-start(f32[19]{0:T(128)} %get-tuple-element.108) | copy-start | bytes 232
  93.5 53.7 %copy-start.10 = (f32[512]{0:T(512)S(1)}, f32[512]{0:T(512)}, u32[]{:S(2)}) copy-start(f32[512]{0:T(512)} %get-tuple-element.106) | copy-start | bytes 6148
  93.5 53.7 %copy-start.11 = (f32[64]{0:T(128)S(1)}, f32[64]{0:T(128)}, u32[]{:S(2)}) copy-start(f32[64]{0:T(128)} %get-tuple-element.83) | copy-start | bytes 772
  93.5 53.7 %copy-start.16 = (f32[64]{0:T(128)S(1)}, f32[64]{0:T(128)}, u32[]{:S(2)}) copy-start(f32[64]{0:T(128)} %get-tuple-element.104) | copy-start | bytes 772
Sparse Core Ops, SparseCore 0:
  82.2 166.6 all-reduce.4

commit v2 on v1

v2 whole, which is shorter than its diff:
```python
import functools

import jax
import jax.numpy as jnp
from jax import lax
from jax.experimental import pallas as pl
from jax.experimental.pallas import tpu as pltpu
from jax.sharding import PartitionSpec as P

GAMMA_THREE = 0.970299
ACTIONS = 18
FLAT = 3136
HIDDEN = 512
CHUNKS = 11
MESH = pl.DeviceIdType.MESH
F32=jnp.float32; BF=jnp.bfloat16
NN=(((1,),(0,)),((),())); NT=(((1,),(1,)),((),())); TN=(((0,),(0,)),((),()))

def dot(a,b,dims=NN):
    return lax.dot_general(a,b,dims,preferred_element_type=F32)
def iota(shape,axis): return lax.broadcasted_iota(jnp.int32,shape,axis)
def tile_lanes(w,width,times,keep,dims=NN):
    n=width*times
    e=((iota((width,n),1)%width==iota((width,n),0)) & (iota((width,n),1)<keep*width)).astype(BF)
    return dot(w,e,dims)

def build_toeplitz(w1,w2,w3,t1,t2a,t2b,t2c,t3a,t3b,u2,u3):
    lane32=iota((16,256),1)//32
    wt1=tile_lanes(w1[...],32,8,7)
    for kr in range(8):
        lo=wt1[32*kr:32*kr+16]; hi=wt1[32*kr+16:32*kr+32]
        for b in range(8):
            t1[pl.ds(128*kr+16*b,16),:]=(jnp.where(lane32==b,lo,0.0)+jnp.where(lane32==b-1,hi,0.0)).astype(BF)
    lane64=iota((32,256),1)//64
    wt2=tile_lanes(w2[...],64,4,4)
    def blk2(kr,p,n,cl):
        col=7*p+cl
        out=jnp.zeros((32,256),F32)
        if cl>=(7 if p<2 else 6): return out
        for kc in range(4):
            if (col-kc)%2: continue
            j=(col-kc)//2
            if 0<=j<9 and 4*n<=j<4*n+4:
                out=out+jnp.where(lane64==j-4*n,wt2[(4*kr+kc)*32:(4*kr+kc)*32+32],0.0)
        return out
    for kr in range(4):
        for cl in range(8):
            for ref,pairs in ((t2a,((0,0),(1,0))),(t2b,((1,1),(2,1)))):
                for k,(p,n) in enumerate(pairs):
                    ref[pl.ds(512*kr+256*k+32*cl,32),:]=blk2(kr,p,n,cl).astype(BF)
            t2c[pl.ds(256*kr+32*cl,32),:]=blk2(kr,2,2,cl)[:,:128].astype(BF)
    lane64b=iota((64,256),1)//64
    wt3=tile_lanes(w3[...],64,4,4)
    def blk3(kr,t,m,cl):
        col=4*t+cl
        out=jnp.zeros((64,256),F32)
        if col>8: return out
        for kc in range(3):
            j=col-kc
            if 0<=j<7 and 4*m<=j<4*m+4:
                out=out+jnp.where(lane64b==j-4*m,wt3[(3*kr+kc)*64:(3*kr+kc)*64+64],0.0)
        return out
    for kr in range(3):
        for cl in range(4):
            t3a[pl.ds(512*kr+64*cl,64),:]=blk3(kr,0,0,cl).astype(BF)
            t3a[pl.ds(512*kr+256+64*cl,64),:]=blk3(kr,1,0,cl).astype(BF)
            t3b[pl.ds(384*kr+64*cl,64),:]=blk3(kr,1,1,cl).astype(BF)
            if cl<2:
                t3b[pl.ds(384*kr+256+64*cl,64),:]=blk3(kr,2,1,cl).astype(BF)
    lane32c=iota((64,256),1)//32
    wx2=[[tile_lanes(w2[pl.ds((4*kr+kc)*32,32),:],32,8,8,TN) for kc in range(4)] for kr in range(4)]
    def ublk2(kr,p,j):
        out=jnp.zeros((64,256),F32)
        if j>8: return out
        for kc in range(4):
            cl=2*j+kc-7*p
            if 0<=cl<(7 if p<2 else 6):
                out=out+jnp.where(lane32c==cl,wx2[kr][kc],0.0)
        return out
    for par in range(2):
        for k2 in range(2):
            kr=par+2*k2
            for jl in range(4):
                u2[par,pl.ds(256*k2+64*jl,64),:]=ublk2(kr,0,jl).astype(BF)
            for j in range(8):
                u2[par,pl.ds(512+512*k2+64*j,64),:]=ublk2(kr,1,j).astype(BF)
            for jl in range(6):
                u2[par,pl.ds(1536+384*k2+64*jl,64),:]=ublk2(kr,2,4+jl).astype(BF)
    wx3=[[tile_lanes(w3[pl.ds((3*kr+kc)*64,64),:],64,4,4,TN) for kc in range(3)] for kr in range(3)]
    def ublk3(kr,t,j):
        out=jnp.zeros((64,256),F32)
        if j>6: return out
        for kc in range(3):
            cl=j+kc-4*t
            if 0<=cl<4 and j+kc<=8:
                out=out+jnp.where(lane64b==cl,wx3[kr][kc],0.0)
        return out
    for kr in range(3):
        for jl in range(4):
            u3[pl.ds(256*kr+64*jl,64),:]=ublk3(kr,0,jl).astype(BF)
        for j in range(8):
            u3[pl.ds(768+512*kr+64*j,64),:]=ublk3(kr,1,j).astype(BF)
        for jl in range(4):
            u3[pl.ds(2304+256*kr+64*jl,64),:]=ublk3(kr,2,4+jl).astype(BF)

def gates(pre):
    s=1.0/(1.0+jnp.exp(-pre))
    return pre*s, s*(1.0+pre*(1.0-s))

def relayout(x, x3, base):
    keep = iota((128, 128), 1) < 112
    for r in range(8):
        for p in range(3):
            at = r * 336 + 112 * p
            if at + 128 <= 2688:
                v = x[at:at + 128, :]
            else:
                v = jnp.concatenate([x[at:2688, :], jnp.zeros((at + 128 - 2688, 128), BF)], 0)
            v = v.T
            if p == 2:
                v = jnp.where(keep, v, jnp.zeros_like(v))
            x3[base + r, :, 128 * p:128 * p + 128] = v

def conv1_rows(c,x3,t1,bias,a1,s1):
    L=[]
    for q in range(2):
        for p in range(3):
            L.append(jnp.concatenate([x3[8*c+4*q+kr,:,128*p:128*p+128] for kr in range(8)],axis=1))
    pre=dot(jnp.concatenate(L,axis=0),t1[...])+bias[:,0:256]
    act,slope=gates(pre)
    for q in range(2):
        for p in range(3):
            k=(3*q+p)*128
            a1[2*c+q,:,256*p:256*p+256]=act[k:k+128].astype(BF)
            s1[2*c+q,:,256*p:256*p+256]=slope[k:k+128]

def conv2_all(a1,t2a,t2b,t2c,bias,a2,s2):
    def step(s,_):
        rows=[[a1[2*(3*s+q)+kr+1] for kr in range(4)] for q in range(3)]
        def lhs(lo,hi):
            return jnp.concatenate([jnp.concatenate([rows[q][kr][:,lo:hi] for kr in range(4)],1) for q in range(3)],0)
        for (lo,hi,w,o0,o1) in ((0,512,t2a,0,256),(256,768,t2b,256,512),(512,768,t2c,512,640)):
            pre=dot(lhs(lo,hi),w[...])+bias[:,256+o0:256+o1]
            act,slope=gates(pre)
            for q in range(3):
                a2[3*s+q,:,o0:o1]=act[128*q:128*q+128].astype(BF)
                s2[3*s+q,:,o0:o1]=slope[128*q:128*q+128]
        return 0
    lax.fori_loop(0,3,step,0)

def conv3_all(a2,t3a,t3b,bias,a3,s3):
    for i0,n in ((0,4),(4,3)):
        for lo,hi,w,o0 in ((0,512,t3a,0),(256,640,t3b,256)):
            L=jnp.concatenate([jnp.concatenate([a2[i0+q+kr][:,lo:hi] for kr in range(3)],1) for q in range(n)],0)
            pre=dot(L,w[...])+bias[:,896+o0:896+o0+256]
            act,slope=gates(pre)
            if o0: slope=jnp.where(iota((128*n,256),1)<192,slope,0.0)
            for q in range(n):
                a3[i0+q,:,o0:o0+256]=act[128*q:128*q+128].astype(BF)
                s3[i0+q,:,o0:o0+256]=slope[128*q:128*q+128]

def dense_head(a3,dw,hw,bias):
    pre=bias[:,1408:1920]
    for r in range(7):
        pre=pre+dot(a3[r],dw[pl.ds(448*r,512),:])
    act,slope=gates(pre)
    act4=act.astype(BF)
    head=dot(act4,hw[...],NT)+bias[:,1920:2048]
    return act4,slope,head

def split2(v):
    hi=v.astype(BF); return hi,(v-hi.astype(F32)).astype(BF)
def split3(v):
    hi=v.astype(BF); r=v-hi.astype(F32); mid=r.astype(BF); return hi,mid,(r-mid.astype(F32)).astype(BF)

def td_part(head,meta,local,legal,table,slots,live_slots):
    lane=iota((slots,128),1)
    idx=local[:,4:5].astype(jnp.int32); live=local[:,5:6]
    action=meta[:,0:1].astype(jnp.int32); game=meta[:,1:2].astype(jnp.int32)
    target=meta[:,2:3]; weight=meta[:,3:4]
    pick=lane==idx
    pickb=pick.astype(F32).astype(BF)
    h=None
    for part in split3(head):
        d=dot(pickb,part); h=d if h is None else h+d
    game_pick=(lane==game).astype(F32).astype(BF)
    mask=dot(game_pick,legal,NT)
    counted=jnp.sum(mask,1,keepdims=True)
    centre=jnp.sum(h*mask,1,keepdims=True)/counted
    q=h[:,ACTIONS:ACTIONS+1]+h-centre
    act_pick=(lane==action).astype(F32)
    td=target-jnp.sum(q*act_pick,1,keepdims=True)
    scaled=live*weight
    mag=jnp.abs(td)
    hub=jnp.where(mag<=1.0,0.5*td*td,mag-0.5)
    loss=jnp.sum(scaled*hub,0,keepdims=True)/live_slots
    gt=-scaled*jnp.clip(td,-1.0,1.0)/live_slots
    G=(gt*(act_pick+(lane==ACTIONS).astype(F32))-mask*(gt/counted)).astype(BF)
    pr=live*jnp.exp(0.3*jnp.log(td*td+1.0))
    fresh=jnp.max(jnp.where(pick,pr,0.0),0,keepdims=True)
    newt=jnp.where(fresh>0.0,fresh,table)
    top=jnp.max(newt,1,keepdims=True)
    grow=dot(pickb,G,TN)
    dhb=jnp.sum(G.astype(F32),0,keepdims=True)
    return q,grow,dhb,loss,newt,top

def head_grads(grow,act4,slope4,hw):
    hi,lo=split2(grow)
    up4=dot(hi,hw[...])+dot(lo,hw[...])
    dhw=dot(hi,act4,TN)+dot(lo,act4,TN)
    g4=(up4*slope4).astype(BF)
    return g4,dhw

def g3_all(g4,dw,s3,g3):
    z=jnp.zeros((128,512),BF)
    for r in (0,1,9,10): g3[r]=z
    b3=None
    for r in range(7):
        up=dot(g4,dw[pl.ds(448*r,512),:],NT)
        g=(up*s3[r]).astype(BF)
        g3[r+2]=g
        b=g.astype(F32); b3=b if b3 is None else b3+b
    return jnp.sum(b3,0,keepdims=True)

def fold64(row):
    n=row.shape[1]//128
    t=row[:,0:128]
    for k in range(1,n): t=t+row[:,128*k:128*k+128]
    return t+pltpu.roll(t,64,1)

def conv3_dw(a2,g3,sp,base):
    low=iota((64,128),1)<64
    G=jnp.concatenate([g3[r+2] for r in range(7)],0)
    def lhs(lo,hi):
        return jnp.concatenate([jnp.concatenate([a2[i+kr][:,lo:hi] for kr in range(3)],1) for i in range(7)],0)
    d0=dot(G[:,0:256],lhs(0,512),TN)
    d1=dot(G[:,256:512],lhs(256,640),TN)
    for kr in range(3):
        E0=E1=O0=O1=None
        for j in range(7):
            def T(ct):
                if j<4: return d0[64*j:64*j+64,512*kr+128*ct:512*kr+128*ct+128]
                return d1[64*(j-4):64*(j-4)+64,384*kr+128*(ct-2):384*kr+128*(ct-2)+128]
            add=lambda a,b: b if a is None else a+b
            if j%2==0:
                E0=add(E0,T(j//2)); E1=add(E1,T(j//2+1))
            else:
                O0=add(O0,T(j//2)); O1=add(O1,T(j//2+1))
        o0=pltpu.roll(O0,64,1); o1=pltpu.roll(O1,64,1)
        sp[pl.ds(base+128*kr,64),:]=E0+jnp.where(low,o0,o1)
        sp[pl.ds(base+128*kr+64,64),:]=E1+o1

def conv3_dx(g3,u3,s2,g2):
    z=jnp.zeros((128,640),BF)
    g2[0]=z; g2[10]=z
    def step(s,tot):
        rows=[[g3[3*s+q+2-kr] for kr in range(3)] for q in range(3)]
        def lhs(lo,hi):
            return jnp.concatenate([jnp.concatenate([rows[q][kr][:,lo:hi] for kr in range(3)],1) for q in range(3)],0)
        outs=[]
        for (lo,hi,k0,k1,o0,o1) in ((0,256,0,768,0,256),(0,512,768,2304,256,512),(256,512,2304,3072,512,640)):
            up=dot(lhs(lo,hi),u3[pl.ds(k0,k1-k0),0:o1-o0])
            acc=None
            for q in range(3):
                g=(up[128*q:128*q+128]*s2[3*s+q,:,o0:o1]).astype(BF)
                g2[3*s+q+1,:,o0:o1]=g
                f=g.astype(F32); acc=f if acc is None else acc+f
            outs.append(jnp.sum(acc,0,keepdims=True))
        return tot+jnp.concatenate(outs,1)
    return lax.fori_loop(0,3,step,jnp.zeros((1,640),F32))

def conv2_dw(a1,g2,sp,base):
    lane=iota((64,128),1)//32
    G=jnp.concatenate([g2[i+1] for i in range(9)],0)
    for kr in range(4):
        L=jnp.concatenate([a1[2*i+kr+1] for i in range(9)],0)
        d=[dot(G[:,0:256],L[:,0:512],TN),dot(G[:,256:512],L[:,256:768],TN),dot(G[:,512:640],L[:,512:768],TN)]
        lo=[0,1,2]
        tot=jnp.zeros((64,128),F32)
        for j in range(9):
            n=j//4
            kc=0
            while kc<4:
                col=2*j+kc; p=min(col//7,2); cl=col-7*p
                lim=7 if p<2 else 6
                cnt=min(4-kc,lim-cl)
                v=d[n][64*(j-4*n):64*(j-4*n)+64,256*(p-lo[n]):256*(p-lo[n])+256]
                sh=(32*(kc-cl))%256
                if sh: v=pltpu.roll(v,sh,1)
                v=v[:,0:128]
                tot=tot+(v if cnt==4 else jnp.where((lane>=kc)&(lane<kc+cnt),v,0.0))
                kc+=cnt
        sp[pl.ds(base+64*kr,64),:]=tot

def conv2_dx(g2,u2,s1,g1):
    def step(t,tot):
        a0=5*(t//2); par=t%2
        def lhs(lo,hi):
            return jnp.concatenate([jnp.concatenate([g2[a0+q+1][:,lo:hi],g2[a0+q][:,lo:hi]],1) for q in range(5)],0)
        outs=[]
        for p,(lo,hi,k0,k1) in enumerate(((0,256,0,512),(0,512,512,1536),(256,640,1536,2304))):
            up=dot(lhs(lo,hi),u2[par,pl.ds(k0,k1-k0),:])
            acc=None
            for q in range(5):
                r=2*(a0+q)+par
                g=(up[128*q:128*q+128]*s1[r+1,:,256*p:256*p+256]).astype(BF)
                g1[r+1,:,256*p:256*p+256]=g
                f=g.astype(F32); acc=f if acc is None else acc+f
            outs.append(jnp.sum(acc,0,keepdims=True))
        return tot+outs[0]+outs[1]+outs[2]
    return lax.fori_loop(0,4,step,jnp.zeros((1,256),F32))

def conv1_dw(x3,g1,acc,sp,base):
    acc[...]=jnp.zeros_like(acc)
    def step(s,_):
        Ls=[];Gs=[]
        for q in range(4):
            for p in range(3):
                Gs.append(g1[4*s+q+1,:,256*p:256*p+256])
                Ls.append(jnp.concatenate([x3[4*(4*s+q)+kr+4,:,128*p:128*p+128] for kr in range(8)],axis=1))
        acc[...]+=dot(jnp.concatenate(Gs,0),jnp.concatenate(Ls,0),TN)
        return 0
    lax.fori_loop(0,5,step,0)
    lane=iota((32,128),1)//32
    for a in range(2):
        out=jnp.zeros((32,128),F32)
        for qq in range(4):
            kr=4*a+qq
            tot=None
            for j in range(7):
                v=acc[pl.ds(32*j,32),128*kr:128*kr+128]
                sh=(32*qq-16*j)%128
                if sh: v=pltpu.roll(v,sh,1)
                tot=v if tot is None else tot+v
            out=out+jnp.where(lane==qq,tot,0.0)
        sp[pl.ds(base+32*a,32),:]=out


def expand_bias(pack, bias):
    def tiled(width):
        e = (iota((128, 256), 1) % width == iota((128, 256), 0)).astype(F32).astype(BF)
        return dot(pack[...], e)
    lane = iota((1, 256), 1)
    zero = jnp.zeros((1, 256), F32)
    t32, t64 = tiled(32), tiled(64)
    bias[:, 0:256] = jnp.where(lane < 224, t32[0:1], zero)
    bias[:, 256:512] = t64[1:2]
    bias[:, 512:768] = t64[1:2]
    bias[:, 768:896] = jnp.where(lane < 64, t64[1:2], zero)[:, 0:128]
    bias[:, 896:1152] = t64[2:3]
    bias[:, 1152:1408] = jnp.where(lane < 192, t64[2:3], zero)
    wide = pack[...].astype(F32)
    for k in range(5):
        bias[:, 1408 + 128 * k:1536 + 128 * k] = wide[3 + k:4 + k]


def prepare_heads(value, advantage, legal, stage, head_w, legal_t):
    stage[...] = jnp.zeros_like(stage)
    stage[0:ACTIONS, :] = advantage[...].astype(F32)
    stage[ACTIONS:ACTIONS + 1, :] = value[...].astype(F32)
    head_w[...] = stage[...].astype(BF)
    stage[...] = jnp.zeros_like(stage)
    stage[0:ACTIONS, 0:legal.shape[1]] = legal[...].astype(F32)
    row = iota((128, 128), 0)
    legal_t[...] = jnp.where(row == 0, 1.0, stage[:, 0:128]).astype(BF)


def prepare_meta(act, game, ret, boot, weight, index, count, stage, meta_out):
    cap, peers = act.shape
    stage[:, 0:128] = jnp.zeros((128, 128), F32)
    fields = (
        act[...].astype(F32),
        game[...].astype(F32),
        ret[...] + GAMMA_THREE * boot[...],
        weight[...],
        index[...].astype(F32),
        (iota((cap, peers), 0) < count[...]).astype(F32),
    )
    for k, field in enumerate(fields):
        stage[8 * k:8 * k + cap, 0:peers] = field
    by_peer = stage[:, 0:128].T
    rows = 8 * peers
    repeat = (iota((rows, 128), 1) == iota((rows, 128), 0) // 8).astype(F32).astype(BF)
    spread = sum(dot(repeat, part) for part in split3(by_peer))
    spread = jnp.where(iota((rows, 128), 0) % 8 == iota((rows, 128), 1) % 8, spread, 0.0)
    collect = (iota((128, 128), 0) // 8 == iota((128, 128), 1)).astype(F32).astype(BF)
    meta_out[...] = sum(dot(part, collect) for part in split3(spread))


def learner_kernel(
    sizes,
    x, act, game, ret, boot, weight, index, count, table, legal, w1, w2, w3, pack, value, advantage, dense_in,
    dg_out, sp_out, q_out, tab_out,
    x3, a1, s1, a2, s2, a3, s3, g3, g2, dw, t1, t2a, t2b, t2c, t3a, t3b, u2, u3, acc,
    bias, stage, head_w, legal_t, meta_out, meta_in, q_send, q_in, a3t, a_in, g4_send, g4_in,
    part, z_in, dg, sp, sp_in, sp_mid, sp_z, sp_all,
    dw_sem, out_sem, meta_s, meta_r, q_s, q_r, a_s, a_r, af_s, af_r, b_s, b_r, rs_s, rs_r,
    az_s, az_r, ap_s, ap_r, ad_s, ad_r, ac_s, ac_r, p1_s, p1_r, p2_s, p2_r, p3_s, p3_r,
):
    hsize, dsize, zrows = sizes
    zsize = dsize // 2
    peers = hsize * dsize
    region = zrows * zsize
    step_at = pl.program_id(0)
    h = lax.axis_index("hst")
    d = lax.axis_index("dev")
    z = d // 2
    core = d % 2
    mine = 2 * h + core
    me = h * dsize + d

    def where_is(peer):
        return (peer // dsize, peer % dsize)

    def send(src, dst, s_sem, r_sem, device):
        copy = pltpu.make_async_remote_copy(
            src_ref=src, dst_ref=dst, send_sem=s_sem, recv_sem=r_sem, device_id=device, device_id_type=MESH
        )
        copy.start()

    def landed(dst, r_sem, s_sem):
        pltpu.make_async_remote_copy(
            src_ref=dst, dst_ref=dst, send_sem=s_sem, recv_sem=r_sem, device_id=(h, d), device_id_type=MESH
        ).wait_recv()

    def sent(src, s_sem, r_sem):
        pltpu.make_async_remote_copy(
            src_ref=src, dst_ref=src, send_sem=s_sem, recv_sem=r_sem, device_id=(h, d), device_id_type=MESH
        ).wait_send()

    @pl.when(step_at == 0)
    def _():
        barrier = pltpu.get_barrier_semaphore()

        def greet(k, carry):
            pl.semaphore_signal(
                barrier, inc=1, device_id=where_is((me + k) % peers), device_id_type=MESH
            )
            return carry

        lax.fori_loop(1, peers, greet, 0)
        pltpu.make_async_copy(dense_in, dw.at[pl.ds(0, FLAT)], dw_sem).start()
        dw[pl.ds(FLAT, 64)] = jnp.zeros((64, HIDDEN), BF)
        build_toeplitz(w1, w2, w3, t1, t2a, t2b, t2c, t3a, t3b, u2, u3)
        expand_bias(pack, bias)
        prepare_heads(value, advantage, legal, stage, head_w, legal_t)
        prepare_meta(act, game, ret, boot, weight, index, count, stage, meta_out)

    relayout(x, x3, 8 * step_at + 4)
    conv1_rows(step_at, x3, t1, bias, a1, s1)

    @pl.when(step_at == 1)
    def _():
        pl.semaphore_wait(pltpu.get_barrier_semaphore(), peers - 1)

        def give(k, carry):
            peer = (me + k) % peers
            send(
                meta_out.at[pl.ds(pl.multiple_of(8 * peer, 8), 8)],
                meta_in.at[pl.ds(pl.multiple_of(8 * me, 8), 8)],
                meta_s.at[k], meta_r.at[k], where_is(peer),
            )
            return carry

        lax.fori_loop(1, peers, give, 0)

    def partial(half):
        for k in range(1, 2 * hsize):
            src = (mine - k + 2 * hsize) % (2 * hsize)
            landed(g4_in.at[half, src], b_r.at[half, k], b_s.at[half, k])
        left = jnp.concatenate([a_in[j] for j in range(2 * hsize)], 1)
        right = jnp.concatenate([g4_in[half, j] for j in range(2 * hsize)], 0)
        part[half, 0:784] = dot(left, right)
        for k in range(1, zsize):
            to = (z + k) % zsize
            send(
                part.at[half, pl.ds(pl.multiple_of(zrows * to, 16), zrows)], z_in.at[half, z],
                rs_s.at[half, k], rs_r.at[half, k], (h, 2 * to + core),
            )
        z_in[half, z] = part[half, pl.ds(pl.multiple_of(zrows * z, 16), zrows)]

    last = step_at == CHUNKS - 1
    sibling = (h, 2 * z + 1 - core)
    own_rows = pl.ds(pl.multiple_of(784 * h, 16), 784)
    row_me = pl.ds(pl.multiple_of(8 * me, 8), 8)

    @pl.when(last)
    def _():
        conv2_all(a1, t2a, t2b, t2c, bias, a2, s2)
        conv3_all(a2, t3a, t3b, bias, a3, s3)
        for r in range(7):
            a3t[pl.ds(448 * r, 448), :] = a3[r].T[0:448]

        for k in range(1, hsize):
            to = (h + k) % hsize
            send(
                a3t.at[pl.ds(pl.multiple_of(784 * to, 16), 784)], a_in.at[mine], a_s.at[k], a_r.at[k], (to, d)
            )
        send(a3t.at[own_rows], a_in.at[mine], af_s.at[0], af_r.at[0], sibling)

    @pl.when(last)
    def _():
        pltpu.make_async_copy(dense_in, dw.at[pl.ds(0, FLAT)], dw_sem).wait()
        act4, slope4, head = dense_head(a3, dw, head_w, bias)

        def take(k, carry):
            peer = (me - k + peers) % peers
            landed(meta_in.at[pl.ds(pl.multiple_of(8 * peer, 8), 8)], meta_r.at[k], meta_s.at[k])
            return carry

        lax.fori_loop(1, peers, take, 0)
        meta_in[row_me, :] = meta_out[row_me, :]
        q, grow, dhb, loss, newt, top = td_part(
            head, meta_in[...], meta_out[...], legal_t[...], table[...], 8 * peers, float(sizes_slots(sizes, act))
        )
        tab_out[...] = jnp.broadcast_to(newt, (8, 128))
        lane = iota((8 * peers, 128), 1)
        q_send[...] = jnp.where(lane == 19, top, jnp.where(lane == 20, loss, q))
        g4, dhw = head_grads(grow, act4, slope4, head_w)
        for quarter in range(4):
            g4_send[quarter] = g4[:, 128 * quarter:128 * quarter + 128]
        for half in range(2):
            for k in range(1, 2 * hsize):
                to = (mine + k) % (2 * hsize)
                send(
                    g4_send.at[2 * (to % 2) + half], g4_in.at[half, mine], b_s.at[half, k], b_r.at[half, k],
                    (to // 2, 2 * z + to % 2),
                )
        for half in range(2):
            g4_in[half, mine] = g4_send[2 * core + half]
        a_in[mine] = a3t[own_rows, :]

        def answer(k, carry):
            peer = (me + k) % peers
            send(
                q_send.at[pl.ds(pl.multiple_of(8 * peer, 8), 8)],
                q_in.at[pl.ds(pl.multiple_of(8 * me, 8), 8)],
                q_s.at[k], q_r.at[k], where_is(peer),
            )
            return carry

        lax.fori_loop(1, peers, answer, 0)
        q_in[row_me, :] = q_send[row_me, :]

        for k in range(4):
            sp[pl.ds(704 + 24 * k, 24), :] = dhw[0:24, 128 * k:128 * k + 128]
        b4 = jnp.sum(g4.astype(F32), 0, keepdims=True)
        for k in range(4):
            sp[803 + k:804 + k, :] = b4[:, 128 * k:128 * k + 128]
        sp[807:808, :] = dhb
        sp[808:832, :] = jnp.zeros((24, 128), F32)
        sp[802:803, :] = fold64(g3_all(g4, dw, s3, g3))

    @pl.when(last)
    def _():
        conv3_dw(a2, g3, sp, 320)

    @pl.when(last)
    def _():
        sp[801:802, :] = fold64(conv3_dx(g3, u3, s2, g2))

        for k in range(1, hsize):
            src = 2 * ((h - k + hsize) % hsize) + core
            landed(a_in.at[src], a_r.at[k], a_s.at[k])
            send(a_in.at[src], a_in.at[src], af_s.at[k], af_r.at[k], sibling)

    @pl.when(last)
    def _():
        conv2_dw(a1, g2, sp, 64)

    @pl.when(last)
    def _():

        for k in range(hsize):
            src = 2 * ((h - k + hsize) % hsize) + 1 - core
            landed(a_in.at[src], af_r.at[k], af_s.at[k])

        for half in range(2):
            part[half, 784:region] = jnp.zeros((region - 784, 128), F32)
        partial(0)

    @pl.when(last)
    def _():
        b1 = conv2_dx(g2, u2, s1, a1)
        b1 = b1[:, 0:128] + b1[:, 128:256]
        b1 = b1 + pltpu.roll(b1, 64, 1)
        sp[800:801, :] = b1 + pltpu.roll(b1, 32, 1)

    @pl.when(last)
    def _():
        partial(1)

    @pl.when(last)
    def _():
        conv1_dw(x3, a1, acc, sp, 0)

    @pl.when(last)
    def _():

        group = 832 // (2 * hsize)

        def group_rows(j):
            return pl.ds(pl.multiple_of(group * j, 8), group)

        for k in range(1, 2 * hsize):
            to = (mine + k) % (2 * hsize)
            send(sp.at[group_rows(to)], sp_in.at[mine], p1_s.at[k], p1_r.at[k], (to // 2, 2 * z + to % 2))

        hy, hx = h // 2, h % 2
        flip_x, flip_y = 2 * hy + 1 - hx, 2 * (1 - hy) + hx
        near = (1 - core) * flip_x + core * flip_y
        far = (1 - core) * flip_y + core * flip_x
        across = 3 - h

        def place(half, hh, zz, cc):
            rows = pl.multiple_of(region * hh + zrows * zz, 16)
            lanes = pl.multiple_of(256 * cc + 128 * half, 128)
            return dg.at[pl.ds(rows, zrows), pl.ds(lanes, 128)]

        def spread(half, zz, k):
            at = place(half, h, zz, core)
            send(at, at, ap_s.at[half, 0, k], ap_r.at[half, 0, k], (near, d))
            send(at, at, ap_s.at[half, 1, k], ap_r.at[half, 1, k], (far, d))
            send(at, at, ac_s.at[half, 0, k], ac_r.at[half, 0, k], sibling)

        def finish(half):
            for k in range(1, zsize):
                landed(z_in.at[half, (z - k + zsize) % zsize], rs_r.at[half, k], rs_s.at[half, k])
            total = z_in[half, 0]
            for j in range(1, zsize):
                total = total + z_in[half, j]
            rows = pl.multiple_of(region * h + zrows * z, 16)
            lanes = pl.multiple_of(256 * core + 128 * half, 128)
            dg[pl.ds(rows, zrows), pl.ds(lanes, 128)] = total.astype(BF)
            at = place(half, h, z, core)
            for k in range(1, zsize):
                send(at, at, az_s.at[half, k], az_r.at[half, k], (h, 2 * ((z + k) % zsize) + core))
            spread(half, z, 0)

        def pass_on(half):
            for k in range(1, zsize):
                zz = (z - k + zsize) % zsize
                landed(place(half, h, zz, core), az_r.at[half, k], az_s.at[half, k])
                spread(half, zz, k)

        def pass_across(half):
            for k in range(zsize):
                zz = (z - k + zsize) % zsize
                at = place(half, near, zz, core)
                landed(at, ap_r.at[half, 0, k], ap_s.at[half, 0, k])
                send(at, at, ad_s.at[half, k], ad_r.at[half, k], (far, d))
                send(at, at, ac_s.at[half, 1, k], ac_r.at[half, 1, k], sibling)
                at = place(half, far, zz, core)
                landed(at, ap_r.at[half, 1, k], ap_s.at[half, 1, k])
                send(at, at, ac_s.at[half, 2, k], ac_r.at[half, 2, k], sibling)

        def pass_last(half):
            for k in range(zsize):
                zz = (z - k + zsize) % zsize
                at = place(half, across, zz, core)
                landed(at, ad_r.at[half, k], ad_s.at[half, k])
                send(at, at, ac_s.at[half, 3, k], ac_r.at[half, 3, k], sibling)

        def gather_core(half):
            other = 1 - core
            near_o = core * flip_x + (1 - core) * flip_y
            far_o = core * flip_y + (1 - core) * flip_x
            for k in range(zsize):
                zz = (z - k + zsize) % zsize
                for j, hh in enumerate((h, near_o, far_o, across)):
                    landed(place(half, hh, zz, other), ac_r.at[half, j, k], ac_s.at[half, j, k])

        finish(0)

        sp_in[mine] = sp[group_rows(mine), :]
        for k in range(1, 2 * hsize):
            src = (mine - k + 2 * hsize) % (2 * hsize)
            landed(sp_in.at[src], p1_r.at[k], p1_s.at[k])
        total = sp_in[0]
        for j in range(1, 2 * hsize):
            total = total + sp_in[j]
        sp_mid[...] = total
        sp_z[z] = total
        for k in range(1, zsize):
            to = (z + k) % zsize
            send(sp_mid, sp_z.at[z], p2_s.at[k], p2_r.at[k], (h, 2 * to + core))

        finish(1)
        pass_on(0)
        for k in range(1, zsize):
            landed(sp_z.at[(z - k + zsize) % zsize], p2_r.at[k], p2_s.at[k])
        total = sp_z[0]
        for j in range(1, zsize):
            total = total + sp_z[j]
        sp_all[group_rows(mine), :] = total
        for k in range(1, 2 * hsize):
            to = (mine + k) % (2 * hsize)
            send(
                sp_all.at[group_rows(mine)], sp_all.at[group_rows(mine)], p3_s.at[k], p3_r.at[k],
                (to // 2, 2 * z + to % 2),
            )
        pass_on(1)
        pass_across(0)
        pass_across(1)
        pass_last(0)
        pass_last(1)
        for k in range(1, 2 * hsize):
            src = (mine - k + 2 * hsize) % (2 * hsize)
            landed(sp_all.at[group_rows(src)], p3_r.at[k], p3_s.at[k])

        def receive(k, carry):
            peer = (me - k + peers) % peers
            landed(q_in.at[pl.ds(pl.multiple_of(8 * peer, 8), 8)], q_r.at[k], q_s.at[k])
            return carry

        lax.fori_loop(1, peers, receive, 0)
        gather_core(0)
        gather_core(1)

        def drain(k, carry):
            sent(meta_out.at[pl.ds(0, 8)], meta_s.at[k], meta_r.at[k])
            sent(q_send.at[pl.ds(0, 8)], q_s.at[k], q_r.at[k])
            return carry

        lax.fori_loop(1, peers, drain, 0)
        for k in range(1, hsize):
            sent(a_in.at[mine], a_s.at[k], a_r.at[k])
        for k in range(hsize):
            sent(a_in.at[mine], af_s.at[k], af_r.at[k])
        for k in range(1, 2 * hsize):
            sent(sp_in.at[mine], p1_s.at[k], p1_r.at[k])
            sent(sp_in.at[mine], p3_s.at[k], p3_r.at[k])
        for k in range(1, zsize):
            sent(sp_mid, p2_s.at[k], p2_r.at[k])
        for half in range(2):
            for k in range(1, 2 * hsize):
                sent(g4_in.at[half, mine], b_s.at[half, k], b_r.at[half, k])
            for k in range(1, zsize):
                sent(z_in.at[half, z], rs_s.at[half, k], rs_r.at[half, k])
                sent(place(half, h, z, core), az_s.at[half, k], az_r.at[half, k])
            for k in range(zsize):
                at = place(half, h, z, core)
                for j in range(2):
                    sent(at, ap_s.at[half, j, k], ap_r.at[half, j, k])
                sent(at, ad_s.at[half, k], ad_r.at[half, k])
                for j in range(4):
                    sent(at, ac_s.at[half, j, k], ac_r.at[half, j, k])

        copies = [
            pltpu.make_async_copy(src, dst, out_sem.at[k])
            for k, (src, dst) in enumerate(((dg, dg_out), (sp_all, sp_out), (q_in, q_out)))
        ]
        for copy in copies:
            copy.start()
        for copy in copies:
            copy.wait()


def sizes_slots(sizes, act):
    return sizes[0] * sizes[1] * act.shape[0]


def learner(sizes, args, cap):
    hsize, dsize, zrows = sizes
    zsize, peers = dsize // 2, hsize * dsize
    region = zrows * zsize
    dma = pltpu.SemaphoreType.DMA
    vmem = pltpu.VMEM
    groups = 2 * hsize
    scratch = [
        vmem((92, 128, 384), BF), vmem((22, 128, 768), BF), vmem((22, 128, 768), F32), vmem((9, 128, 640), BF),
        vmem((9, 128, 640), F32), vmem((7, 128, 512), BF), vmem((7, 128, 512), F32), vmem((11, 128, 512), BF),
        vmem((11, 128, 640), BF), vmem((3200, 512), BF), vmem((1024, 256), BF), vmem((2048, 256), BF),
        vmem((2048, 256), BF), vmem((1024, 128), BF), vmem((1536, 256), BF), vmem((1152, 256), BF),
        vmem((2, 2304, 256), BF), vmem((3072, 256), BF), vmem((256, 1024), F32),
        vmem((1, 2048), F32), vmem((128, 512), F32), vmem((128, 512), BF), vmem((128, 128), BF),
        vmem((8 * peers, 128), F32), vmem((8 * peers, 128), F32), vmem((8 * peers, 128), F32),
        vmem((8 * peers, 128), F32), vmem((FLAT, 128), BF), vmem((groups, 784, 128), BF), vmem((4, 128, 128), BF),
        vmem((2, groups, 128, 128), BF), vmem((2, region, 128), F32), vmem((2, zsize, zrows, 128), F32),
        vmem((hsize * region, 512), BF), vmem((832, 128), F32), vmem((groups, 832 // groups, 128), F32),
        vmem((832 // groups, 128), F32), vmem((zsize, 832 // groups, 128), F32), vmem((832, 128), F32),
        dma, dma((3,)), dma((peers,)), dma((peers,)), dma((peers,)), dma((peers,)),
        dma((hsize,)), dma((hsize,)), dma((hsize,)), dma((hsize,)), dma((2, groups)), dma((2, groups)),
        dma((2, zsize)), dma((2, zsize)), dma((2, zsize)), dma((2, zsize)),
        dma((2, 2, zsize)), dma((2, 2, zsize)), dma((2, zsize)), dma((2, zsize)),
        dma((2, 4, zsize)), dma((2, 4, zsize)), dma((groups,)), dma((groups,)), dma((zsize,)), dma((zsize,)),
        dma((groups,)), dma((groups,)),
    ]
    whole = pl.BlockSpec(memory_space=pltpu.VMEM)
    outside = pl.BlockSpec(memory_space=pl.ANY)
    return pl.pallas_call(
        functools.partial(learner_kernel, sizes),
        grid=(CHUNKS,),
        in_specs=[pl.BlockSpec((2688, 128), lambda c: (c, 0))] + [whole] * 15 + [outside],
        out_specs=[outside, outside, outside, whole],
        out_shape=[
            jax.ShapeDtypeStruct((hsize * region, 512), BF),
            jax.ShapeDtypeStruct((832, 128), F32),
            jax.ShapeDtypeStruct((8 * peers, 128), F32),
            jax.ShapeDtypeStruct((8, 128), F32),
        ],
        scratch_shapes=scratch,
        compiler_params=pltpu.CompilerParams(collective_id=0, has_side_effects=True, vmem_limit_bytes=63 << 20),
    )(*args)


def output_kernel(dg, sp, q, tab, dense, c1, c2, c3, bias1, bias2, bias3, bias4, vw, vb, aw, ab, loss, top, table):
    dense[...] = dg[0:784].astype(F32)

    @pl.when(pl.program_id(0) == 0)
    def _():
        for a in range(2):
            c1[pl.ds(128 * a, 128), :] = sp[pl.ds(32 * a, 32), :].T
        for kr in range(4):
            c2[pl.ds(128 * kr, 128), :] = sp[pl.ds(64 + 64 * kr, 64), :].T
        for kr in range(3):
            c3[pl.ds(192 * kr, 128), :] = sp[pl.ds(320 + 128 * kr, 64), :].T
            c3[pl.ds(192 * kr + 128, 64), :] = sp[pl.ds(384 + 128 * kr, 64), :].T[0:64]
        bias1[...] = sp[800:801, 0:32]
        bias2[...] = sp[801:802, 0:64]
        bias3[...] = sp[802:803, 0:64]
        for k in range(4):
            bias4[:, 128 * k:128 * k + 128] = sp[803 + k:804 + k, :]
            heads = sp[pl.ds(704 + 24 * k, 24), :]
            aw[:, 128 * k:128 * k + 128] = heads[0:ACTIONS]
            vw[:, 128 * k:128 * k + 128] = heads[ACTIONS:ACTIONS + 1]
        ab[...] = sp[807:808, 0:ACTIONS]
        vb[...] = sp[807:808, ACTIONS:ACTIONS + 1]
        rows = q[...]
        top[...] = jnp.max(rows[:, 19:20], 0, keepdims=True)
        first = iota((rows.shape[0], 1), 0) % 8 == 0
        loss[...] = jnp.sum(jnp.where(first, rows[:, 20:21], 0.0), 0, keepdims=True)
        table[...] = tab[0:1, :]


def outputs(sizes, dg, sp, q, tab):
    hsize, dsize, zrows = sizes
    region = zrows * (dsize // 2)
    whole = pl.BlockSpec(memory_space=pltpu.VMEM)
    shapes = (
        (FLAT, 512), (256, 32), (512, 64), (576, 64), (1, 32), (1, 64), (1, 64), (1, 512), (1, 512), (1, 1),
        (ACTIONS, 512), (1, ACTIONS), (1, 1), (1, 1), (1, 128),
    )
    return pl.pallas_call(
        output_kernel,
        grid=(hsize,),
        in_specs=[pl.BlockSpec((region, 512), lambda k: (k, 0)), whole, whole, whole],
        out_specs=[pl.BlockSpec((784, 512), lambda k: (k, 0))] + [whole] * 14,
        out_shape=[jax.ShapeDtypeStruct(s, F32) for s in shapes],
    )(dg, sp, q, tab)


def per_device(
    hsize,
    dsize,
    replay,
    send_index,
    send_count,
    actions,
    game_ids,
    legal_table,
    returns,
    bootstrap,
    is_weights,
    priority_table,
    conv1_w,
    conv1_b,
    conv2_w,
    conv2_b,
    conv3_w,
    conv3_b,
    dense_w,
    dense_b,
    value_w,
    value_b,
    advantage_w,
    advantage_b,
):
    cap = send_index.shape[2]
    peers = hsize * dsize
    zsize = dsize // 2
    zrows = -(-784 // (16 * zsize)) * 16
    sizes = (hsize, dsize, zrows)
    gap = functools.partial(jnp.zeros, dtype=BF)
    pack = jnp.concatenate(
        [conv1_b, gap(96), conv2_b, gap(64), conv3_b, gap(64), dense_b, advantage_b, value_b, gap(109)]
    ).reshape(8, 128)
    args = (
        replay.T,
        actions[0].T,
        game_ids[0].T,
        returns[0].T,
        bootstrap[0].T,
        is_weights[0].T,
        send_index[0].T,
        send_count,
        priority_table.reshape(1, -1),
        legal_table.T,
        conv1_w.reshape(256, 32),
        conv2_w.reshape(512, 64),
        conv3_w.reshape(576, 64),
        pack,
        value_w.T,
        advantage_w.T,
        dense_w,
    )
    dg, sp, q, tab = learner(sizes, args, cap)
    (dense, c1, c2, c3, b1, b2, b3, b4, vw, vb, aw, ab, loss, top, table) = outputs(sizes, dg, sp, q, tab)
    q_values = q.reshape(peers, 8, 128)[:, :cap, :ACTIONS].reshape(1, peers * cap, ACTIONS)
    return (
        q_values,
        loss.reshape(()),
        c1.reshape(conv1_w.shape),
        b1.reshape(-1),
        c2.reshape(conv2_w.shape),
        b2.reshape(-1),
        c3.reshape(conv3_w.shape),
        b3.reshape(-1),
        dense,
        b4.reshape(-1),
        vw.T,
        vb.reshape(-1),
        aw.T,
        ab.reshape(-1),
        table.reshape(-1),
        top.reshape(()),
    )


def solution(mesh):
    both = ("hst", "dev")
    rows2, rows3 = P(both, None), P(both, None, None)
    placed = (rows2, rows3, rows2, rows3, rows3, P(), rows3, rows3, rows3, P(both)) + (P(),) * 12
    return jax.shard_map(
        functools.partial(per_device, mesh.shape["hst"], mesh.shape["dev"]),
        mesh=mesh,
        in_specs=placed,
        out_specs=(rows3,) + (P(),) * 13 + (P(both), P()),
        check_vma=False,
    )
```

time: 267 us -> 105 us (0.39)
  Pallas kernels: 0 us -> 97.8 us
  blocking collectives: 83.4 us -> 0 us
  matrix products: 62.4 us -> 0 us
  waiting for transfers between devices: 55.7 us -> 0 us
  other arithmetic: 16.2 us -> 0 us
  between operations: 15.7 us -> 1.34 us
  local copies, waits for them, and re-layouts: 19 us -> 5.64 us
  starting transfers between devices: 13 us -> 0 us
    pallas_call x0 -> x2, Pallas kernels: none -> 97.8 us  [the longest x1 91.9 us: learner(): pl.pallas_call(functools.partial(learner_kernel, sizes), grid=(CHUNKS,),...]
    psum x1 -> x0, waiting for transfers between devices: 55.6 us -> none  [per_device(): totals = lax.psum((loss_local,) + grads, axes)]
    conv_general_dilated x8 -> x0, matrix products: 50.8 us -> none  [the longest x3 19.8 us: forward_conv(): lax.conv_general_dilated(source, kernel, (stride, stride), 'VALID', dimen...]
    psum x1 -> x0, blocking collectives: 43.2 us -> none  [per_device(): totals = lax.psum((loss_local,) + grads, axes)]
    pmax x1 -> x0, blocking collectives: 40.2 us -> none  [per_device(): top_priority = lax.pmax(jnp.max(new_table), axes)]
    unnamed x71 -> x1, local copies, waits for them, and re-layouts: 14.7 us -> 0.69 us
    all_to_all x2 -> x0, starting transfers between devices: 13 us -> none  [the longest x1 7.1 us: per_device(): lax.all_to_all(outgoing, axes, split_axis=0, concat_axis=0, tiled=True)]
    dot_general x9 -> x0, matrix products: 11.6 us -> none  [the longest x1 3.87 us: transposed_dot(): lax.dot_general(left_side, right_side, (((0,), (0,)), ((), ())), preferre...]
  transfers between devices with their start and end apart: 3 -> 0, of which waited for: 1 -> 0; matrix products, arithmetic and copies ran while one was open for 25% -> 0% of each run, Pallas kernels for 0% -> 0%
where the time goes in v2:
time: 105 us
  Pallas kernels  97.8 us (93%)
  local copies, waits for them, and re-layouts  5.64 us (5%)
  between operations  1.34 us (1%)
    pallas_call x1, Pallas kernels, learner(): pl.pallas_call(functools.partial(learner_kernel, sizes), grid=(CHUNKS,),...  91.9 us
    pallas_call x1, Pallas kernels, outputs(): pl.pallas_call(output_kernel, grid=(hsize,), in_specs=[pl.BlockSpec((regi...  5.92 us
    concatenate x1, local copies, waits for them, and re-layouts, per_device(): jnp.concatenate([conv1_b, gap(96), conv2_b, gap(64), conv3_b, gap(64), de...  4.03 us

profile of v2, /device:TPU:1, one launch (start us, length us, event | category | flops | bytes accessed | tf_op | source)
XLA Modules:
  0.0 104.8 jit_solution(10190037619976861975)
XLA Ops:
  1.3 4.0 %concatenate.3 = bf16[1024]{0:T(1024)(128)(2,1)} concatenate(bf16[32]{0:T(256)(128)(2,1)} %param.33, bf16[96]{0:T(256)(128)(2,1)S(1)} %broadcast_in_dim.6, bf16[64]{0:T(256)(128)(2,1)} %param.35, bf16[64]{0:T(256)(128)(2,1)S(1)} %broadcast.3, bf16[64]{0:T(256)(128)(2,1)} %param.37, bf16[64]{0:T(256)(128)(2,1)S(1)} %broadcast.3, bf16[512]{0:T(512)(128)(2,1)} %param.39, ...), dimensions={0} | concatenate | bytes 4096 | tf_op jit(solution)/shard_map/concatenate | solution.py:885
  5.4 91.9 %shard_map.333 = (bf16[3328,512]{1,0:T(8,128)(2,1)}, f32[832,128]{1,0:T(8,128)}, f32[256,128]{1,0:T(8,128)}, f32[8,128]{1,0:T(8,128)}) custom-call(bf16[28224,128]{1,0:T(8,128)(2,1)} %bitcast.44, s32[8,32]{1,0:T(8,128)} %bitcast.52, s32[8,32]{1,0:T(8,128)} %bitcast.53, f32[8,32]{1,0:T(8,128)} %bitcast.54, f32[8,32]{1,0:T(8,128)} %bitcast.55, ...), custom_call_target="tpu_custom_call" | custom-call | tf_op jit(solution)/shard_map/pallas_call | solution.py:791
  97.2 5.9 %shard_map.334 = (f32[3136,512]{1,0:T(8,128)}, f32[256,32]{1,0:T(8,128)}, f32[512,64]{1,0:T(8,128)}, f32[576,64]{1,0:T(8,128)}, f32[1,32]{1,0:T(1,128)}, /*index...) custom-call(bf16[3328,512]{1,0:T(8,128)(2,1)} %get-tuple-element.36., ...), custom_call_target="tpu_custom_call" | custom-call | tf_op jit(solution)/shard_map/pallas_call | solution.py:844
  103.2 0.9 slice_bitcast_fusion
  104.1 0.7 copy.39
  (3 shorter events, 0.0 us)

commit v3 on v2

v3 whole, which is shorter than its diff:
```python
import functools

import jax
import jax.numpy as jnp
from jax import lax
from jax.experimental import pallas as pl
from jax.experimental.pallas import tpu as pltpu
from jax.sharding import PartitionSpec as P

GAMMA_THREE = 0.970299
ACTIONS = 18
FLAT = 3136
HIDDEN = 512
CHUNKS = 11
PIXELS = 2688
SLOTS = 4
MESH = pl.DeviceIdType.MESH
JOIN = (
    "meta", "q", "g4", "sum0", "sum1", "gather_core0", "gather_core1", "small", "small_z", "small_back", "small_all",
    "small_core", "late", "late_z", "late_all",
)
LEAVE = JOIN + (
    "act", "act_core", "gather_z0", "gather_z1", "gather_near0", "gather_near1", "gather_diag0", "gather_diag1",
)
ROWS = (416, 384)
START = (0, 400)
F32=jnp.float32; BF=jnp.bfloat16
NN=(((1,),(0,)),((),())); NT=(((1,),(1,)),((),())); TN=(((0,),(0,)),((),()))

def dot(a,b,dims=NN):
    return lax.dot_general(a,b,dims,preferred_element_type=F32)
def iota(shape,axis): return lax.broadcasted_iota(jnp.int32,shape,axis)
def tile_lanes(w,width,times,keep,dims=NN):
    n=width*times
    e=((iota((width,n),1)%width==iota((width,n),0)) & (iota((width,n),1)<keep*width)).astype(BF)
    return dot(w,e,dims)

def build_toeplitz(w1,w2,w3,t1,t2a,t2b,t2c,t3a,t3b):
    lane32=iota((16,256),1)//32
    wt1=tile_lanes(w1[...],32,8,7)
    for kr in range(8):
        lo=wt1[32*kr:32*kr+16]; hi=wt1[32*kr+16:32*kr+32]
        for b in range(8):
            t1[pl.ds(128*kr+16*b,16),:]=(jnp.where(lane32==b,lo,0.0)+jnp.where(lane32==b-1,hi,0.0)).astype(BF)
    lane64=iota((32,256),1)//64
    wt2=tile_lanes(w2[...],64,4,4)
    def blk2(kr,p,n,cl):
        col=7*p+cl
        out=jnp.zeros((32,256),F32)
        if cl>=(7 if p<2 else 6): return out
        for kc in range(4):
            if (col-kc)%2: continue
            j=(col-kc)//2
            if 0<=j<9 and 4*n<=j<4*n+4:
                out=out+jnp.where(lane64==j-4*n,wt2[(4*kr+kc)*32:(4*kr+kc)*32+32],0.0)
        return out
    for kr in range(4):
        for cl in range(8):
            for ref,pairs in ((t2a,((0,0),(1,0))),(t2b,((1,1),(2,1)))):
                for k,(p,n) in enumerate(pairs):
                    ref[pl.ds(512*kr+256*k+32*cl,32),:]=blk2(kr,p,n,cl).astype(BF)
            t2c[pl.ds(256*kr+32*cl,32),:]=blk2(kr,2,2,cl)[:,:128].astype(BF)
    lane64b=iota((64,256),1)//64
    wt3=tile_lanes(w3[...],64,4,4)
    def blk3(kr,t,m,cl):
        col=4*t+cl
        out=jnp.zeros((64,256),F32)
        if col>8: return out
        for kc in range(3):
            j=col-kc
            if 0<=j<7 and 4*m<=j<4*m+4:
                out=out+jnp.where(lane64b==j-4*m,wt3[(3*kr+kc)*64:(3*kr+kc)*64+64],0.0)
        return out
    for kr in range(3):
        for cl in range(4):
            t3a[pl.ds(512*kr+64*cl,64),:]=blk3(kr,0,0,cl).astype(BF)
            t3a[pl.ds(512*kr+256+64*cl,64),:]=blk3(kr,1,0,cl).astype(BF)
            t3b[pl.ds(384*kr+64*cl,64),:]=blk3(kr,1,1,cl).astype(BF)
            if cl<2:
                t3b[pl.ds(384*kr+256+64*cl,64),:]=blk3(kr,2,1,cl).astype(BF)

def build_transposed(w2,w3,u2,u3):
    lane64b=iota((64,256),1)//64
    lane32c=iota((64,256),1)//32
    wx2=[[tile_lanes(w2[pl.ds((4*kr+kc)*32,32),:],32,8,8,TN) for kc in range(4)] for kr in range(4)]
    def ublk2(kr,p,j):
        out=jnp.zeros((64,256),F32)
        if j>8: return out
        for kc in range(4):
            cl=2*j+kc-7*p
            if 0<=cl<(7 if p<2 else 6):
                out=out+jnp.where(lane32c==cl,wx2[kr][kc],0.0)
        return out
    for par in range(2):
        for k2 in range(2):
            kr=par+2*k2
            for jl in range(4):
                u2[par,pl.ds(256*k2+64*jl,64),:]=ublk2(kr,0,jl).astype(BF)
            for j in range(8):
                u2[par,pl.ds(512+512*k2+64*j,64),:]=ublk2(kr,1,j).astype(BF)
            for jl in range(6):
                u2[par,pl.ds(1536+384*k2+64*jl,64),:]=ublk2(kr,2,4+jl).astype(BF)
    wx3=[[tile_lanes(w3[pl.ds((3*kr+kc)*64,64),:],64,4,4,TN) for kc in range(3)] for kr in range(3)]
    def ublk3(kr,t,j):
        out=jnp.zeros((64,256),F32)
        if j>6: return out
        for kc in range(3):
            cl=j+kc-4*t
            if 0<=cl<4 and j+kc<=8:
                out=out+jnp.where(lane64b==cl,wx3[kr][kc],0.0)
        return out
    for kr in range(3):
        for jl in range(4):
            u3[pl.ds(256*kr+64*jl,64),:]=ublk3(kr,0,jl).astype(BF)
        for j in range(8):
            u3[pl.ds(768+512*kr+64*j,64),:]=ublk3(kr,1,j).astype(BF)
        for jl in range(4):
            u3[pl.ds(2304+256*kr+64*jl,64),:]=ublk3(kr,2,4+jl).astype(BF)

def gates(pre):
    s=1.0/(1.0+jnp.exp(-pre))
    return pre*s, s*(1.0+pre*(1.0-s))

def relayout(x, x3, base, rows=8):
    keep = iota((128, 128), 1) < 112
    for r in range(rows):
        for p in range(3):
            at = r * 336 + 112 * p
            if at + 128 <= 336 * rows:
                v = x[at:at + 128, :]
            else:
                v = jnp.concatenate([x[at:336 * rows, :], jnp.zeros((at + 128 - 336 * rows, 128), BF)], 0)
            v = v.T
            if p == 2:
                v = jnp.where(keep, v, jnp.zeros_like(v))
            x3[base + r, :, 128 * p:128 * p + 128] = v

def conv1_rows(c,x3,t1,bias,a1,s1,which=(0,1)):
    L=[]
    for q in which:
        for p in range(3):
            L.append(jnp.concatenate([x3[8*c+4*q+kr,:,128*p:128*p+128] for kr in range(8)],axis=1))
    pre=dot(jnp.concatenate(L,axis=0),t1[...])+bias[:,0:256]
    act,slope=gates(pre)
    for q in which:
        for p in range(3):
            k=(3*(q-which[0])+p)*128
            a1[2*c+q,:,256*p:256*p+256]=act[k:k+128].astype(BF)
            s1[2*c+q,:,256*p:256*p+256]=slope[k:k+128]

def conv2_all(a1,t2a,t2b,t2c,bias,a2,s2):
    rows=[[a1[2*(q)+kr+1] for kr in range(4)] for q in range(9)]
    def lhs(lo,hi):
        return jnp.concatenate([jnp.concatenate([rows[q][kr][:,lo:hi] for kr in range(4)],1) for q in range(9)],0)
    for (lo,hi,w,o0,o1) in ((0,512,t2a,0,256),(256,768,t2b,256,512),(512,768,t2c,512,640)):
        pre=dot(lhs(lo,hi),w[...])+bias[:,256+o0:256+o1]
        act,slope=gates(pre)
        for q in range(9):
            a2[q,:,o0:o1]=act[128*q:128*q+128].astype(BF)
            s2[q,:,o0:o1]=slope[128*q:128*q+128]

def conv3_all(a2,t3a,t3b,bias,a3,s3):
    for i0,n in ((0,4),(4,3)):
        for lo,hi,w,o0 in ((0,512,t3a,0),(256,640,t3b,256)):
            L=jnp.concatenate([jnp.concatenate([a2[i0+q+kr][:,lo:hi] for kr in range(3)],1) for q in range(n)],0)
            pre=dot(L,w[...])+bias[:,896+o0:896+o0+256]
            act,slope=gates(pre)
            if o0: slope=jnp.where(iota((128*n,256),1)<192,slope,0.0)
            for q in range(n):
                a3[i0+q,:,o0:o0+256]=act[128*q:128*q+128].astype(BF)
                s3[i0+q,:,o0:o0+256]=slope[128*q:128*q+128]

def dense_head(a3,dw,hw,bias):
    pre=bias[:,1408:1920]
    for r in range(7):
        pre=pre+dot(a3[r],dw[pl.ds(448*r,512),:])
    act,slope=gates(pre)
    act4=act.astype(BF)
    head=dot(act4,hw[...],NT)+bias[:,1920:2048]
    return act4,slope,head

def split2(v):
    hi=v.astype(BF); return hi,(v-hi.astype(F32)).astype(BF)
def split3(v):
    hi=v.astype(BF); r=v-hi.astype(F32); mid=r.astype(BF); return hi,mid,(r-mid.astype(F32)).astype(BF)

def td_part(head,meta,local,legal,table,slots,live_slots):
    lane=iota((slots,128),1)
    idx=local[:,4:5].astype(jnp.int32); live=local[:,5:6]
    action=meta[:,0:1].astype(jnp.int32); game=meta[:,1:2].astype(jnp.int32)
    target=meta[:,2:3]; weight=meta[:,3:4]
    pick=lane==idx
    pickb=pick.astype(F32).astype(BF)
    h=None
    for part in split3(head):
        d=dot(pickb,part); h=d if h is None else h+d
    game_pick=(lane==game).astype(F32).astype(BF)
    mask=dot(game_pick,legal,NT)
    counted=jnp.sum(mask,1,keepdims=True)
    centre=jnp.sum(h*mask,1,keepdims=True)/counted
    q=h[:,ACTIONS:ACTIONS+1]+h-centre
    act_pick=(lane==action).astype(F32)
    td=target-jnp.sum(q*act_pick,1,keepdims=True)
    scaled=live*weight
    mag=jnp.abs(td)
    hub=jnp.where(mag<=1.0,0.5*td*td,mag-0.5)
    loss=jnp.sum(scaled*hub,0,keepdims=True)/live_slots
    gt=-scaled*jnp.clip(td,-1.0,1.0)/live_slots
    G=(gt*(act_pick+(lane==ACTIONS).astype(F32))-mask*(gt/counted)).astype(BF)
    pr=live*jnp.exp(0.3*jnp.log(td*td+1.0))
    fresh=jnp.max(jnp.where(pick,pr,0.0),0,keepdims=True)
    newt=jnp.where(fresh>0.0,fresh,table)
    top=jnp.max(newt,1,keepdims=True)
    grow=dot(pickb,G,TN)
    dhb=jnp.sum(G.astype(F32),0,keepdims=True)
    return q,grow,dhb,loss,newt,top

def head_grads(grow,act4,slope4,hw):
    hi,lo=split2(grow)
    up4=dot(hi,hw[...])+dot(lo,hw[...])
    dhw=dot(hi,act4,TN)+dot(lo,act4,TN)
    g4=(up4*slope4).astype(BF)
    return g4,dhw

def g3_all(g4,dw,s3,g3):
    z=jnp.zeros((128,512),BF)
    for r in (0,1,9,10): g3[r]=z
    b3=None
    for r in range(7):
        up=dot(g4,dw[pl.ds(448*r,512),:],NT)
        g=(up*s3[r]).astype(BF)
        g3[r+2]=g
        b=g.astype(F32); b3=b if b3 is None else b3+b
    return jnp.sum(b3,0,keepdims=True)

def fold64(row):
    n=row.shape[1]//128
    t=row[:,0:128]
    for k in range(1,n): t=t+row[:,128*k:128*k+128]
    return t+pltpu.roll(t,64,1)

def conv3_dw(a2,g3,sp,base):
    low=iota((64,128),1)<64
    G=jnp.concatenate([g3[r+2] for r in range(7)],0)
    def lhs(lo,hi):
        return jnp.concatenate([jnp.concatenate([a2[i+kr][:,lo:hi] for kr in range(3)],1) for i in range(7)],0)
    d0=dot(G[:,0:256],lhs(0,512),TN)
    d1=dot(G[:,256:512],lhs(256,640),TN)
    for kr in range(3):
        E0=E1=O0=O1=None
        for j in range(7):
            def T(ct):
                if j<4: return d0[64*j:64*j+64,512*kr+128*ct:512*kr+128*ct+128]
                return d1[64*(j-4):64*(j-4)+64,384*kr+128*(ct-2):384*kr+128*(ct-2)+128]
            add=lambda a,b: b if a is None else a+b
            if j%2==0:
                E0=add(E0,T(j//2)); E1=add(E1,T(j//2+1))
            else:
                O0=add(O0,T(j//2)); O1=add(O1,T(j//2+1))
        o0=pltpu.roll(O0,64,1); o1=pltpu.roll(O1,64,1)
        sp[pl.ds(base+128*kr,64),:]=E0+jnp.where(low,o0,o1)
        sp[pl.ds(base+128*kr+64,64),:]=E1+o1

def conv3_dx(g3,u3,s2,g2):
    z=jnp.zeros((128,640),BF)
    g2[0]=z; g2[10]=z
    def step(s,tot):
        rows=[[g3[3*s+q+2-kr] for kr in range(3)] for q in range(3)]
        def lhs(lo,hi):
            return jnp.concatenate([jnp.concatenate([rows[q][kr][:,lo:hi] for kr in range(3)],1) for q in range(3)],0)
        outs=[]
        for (lo,hi,k0,k1,o0,o1) in ((0,256,0,768,0,256),(0,512,768,2304,256,512),(256,512,2304,3072,512,640)):
            up=dot(lhs(lo,hi),u3[pl.ds(k0,k1-k0),0:o1-o0])
            acc=None
            for q in range(3):
                g=(up[128*q:128*q+128]*s2[3*s+q,:,o0:o1]).astype(BF)
                g2[3*s+q+1,:,o0:o1]=g
                f=g.astype(F32); acc=f if acc is None else acc+f
            outs.append(jnp.sum(acc,0,keepdims=True))
        return tot+jnp.concatenate(outs,1)
    return lax.fori_loop(0,3,step,jnp.zeros((1,640),F32))

def conv2_dw(a1,g2,sp,base,first,last):
    lane=iota((64,128),1)//32
    G=jnp.concatenate([g2[i+1] for i in range(9)],0)
    for kr in range(first,last):
        L=jnp.concatenate([a1[2*i+kr+1] for i in range(9)],0)
        d=[dot(G[:,0:256],L[:,0:512],TN),dot(G[:,256:512],L[:,256:768],TN),dot(G[:,512:640],L[:,512:768],TN)]
        lo=[0,1,2]
        tot=jnp.zeros((64,128),F32)
        for j in range(9):
            n=j//4
            kc=0
            while kc<4:
                col=2*j+kc; p=min(col//7,2); cl=col-7*p
                lim=7 if p<2 else 6
                cnt=min(4-kc,lim-cl)
                v=d[n][64*(j-4*n):64*(j-4*n)+64,256*(p-lo[n]):256*(p-lo[n])+256]
                sh=(32*(kc-cl))%256
                if sh: v=pltpu.roll(v,sh,1)
                v=v[:,0:128]
                tot=tot+(v if cnt==4 else jnp.where((lane>=kc)&(lane<kc+cnt),v,0.0))
                kc+=cnt
        sp[pl.ds(base+64*kr,64),:]=tot

def conv2_dx(g2,u2,s1,g1,first,last):
    def step(t,tot):
        a0=5*(t//2); par=t%2
        def lhs(lo,hi):
            return jnp.concatenate([jnp.concatenate([g2[a0+q+1][:,lo:hi],g2[a0+q][:,lo:hi]],1) for q in range(5)],0)
        outs=[]
        for p,(lo,hi,k0,k1) in enumerate(((0,256,0,512),(0,512,512,1536),(256,640,1536,2304))):
            up=dot(lhs(lo,hi),u2[par,pl.ds(k0,k1-k0),:])
            acc=None
            for q in range(5):
                r=2*(a0+q)+par
                g=(up[128*q:128*q+128]*s1[r+1,:,256*p:256*p+256]).astype(BF)
                g1[r+1,:,256*p:256*p+256]=g
                f=g.astype(F32); acc=f if acc is None else acc+f
            outs.append(jnp.sum(acc,0,keepdims=True))
        return tot+outs[0]+outs[1]+outs[2]
    return lax.fori_loop(first,last,step,jnp.zeros((1,256),F32))

def conv1_dw(x3,g1,acc,first,last):
    if first==0: acc[...]=jnp.zeros_like(acc)
    def step(s,_):
        Ls=[];Gs=[]
        for q in range(4):
            for p in range(3):
                Gs.append(g1[4*s+q+1,:,256*p:256*p+256])
                Ls.append(jnp.concatenate([x3[4*(4*s+q)+kr+4,:,128*p:128*p+128] for kr in range(8)],axis=1))
        acc[...]+=dot(jnp.concatenate(Gs,0),jnp.concatenate(Ls,0),TN)
        return 0
    lax.fori_loop(first,last,step,0)

def conv1_fold(acc,sp,base):
    lane=iota((32,128),1)//32
    for a in range(2):
        out=jnp.zeros((32,128),F32)
        for qq in range(4):
            kr=4*a+qq
            tot=None
            for j in range(7):
                v=acc[pl.ds(32*j,32),128*kr:128*kr+128]
                sh=(32*qq-16*j)%128
                if sh: v=pltpu.roll(v,sh,1)
                tot=v if tot is None else tot+v
            out=out+jnp.where(lane==qq,tot,0.0)
        sp[pl.ds(base+32*a,32),:]=out


def to_fixed(v):
    top = jnp.maximum(jnp.max(jnp.abs(v), 0, keepdims=True), 1e-30)
    e = jnp.ceil(jnp.log(top) * 1.4426950408889634)
    code = jnp.clip(jnp.round(v * jnp.exp((15.0 - e) * 0.6931471805599453)), -32767.0, 32767.0)
    return code.astype(jnp.int32).astype(jnp.int16), jnp.broadcast_to(e, (16, 128)).astype(jnp.int32).astype(jnp.int16)

def from_fixed(code, e):
    scale = jnp.exp((e.astype(jnp.int32).astype(F32)[0:1] - 15.0) * 0.6931471805599453)
    return code.astype(jnp.int32).astype(F32) * scale


def expand_bias(raw, stage, pack, bias):
    c1, c2, c3, dense, value, advantage = raw
    stage[...] = jnp.zeros_like(stage)
    stage[0:1, 0:32] = c1[...].astype(F32)
    stage[1:2, 0:64] = c2[...].astype(F32)
    stage[2:3, 0:64] = c3[...].astype(F32)
    stage[3:7, 0:128] = dense[...].astype(F32)
    stage[7:8, 0:ACTIONS] = advantage[...].astype(F32)
    heads = jnp.where(iota((1, 128), 1) == ACTIONS, value[...].astype(F32), stage[7:8, 0:128])
    stage[7:8, 0:128] = heads
    pack[...] = stage[0:8, 0:128].astype(BF)

    def tiled(width):
        e = (iota((128, 256), 1) % width == iota((128, 256), 0)).astype(F32).astype(BF)
        return dot(pack[...], e)
    lane = iota((1, 256), 1)
    zero = jnp.zeros((1, 256), F32)
    t32, t64 = tiled(32), tiled(64)
    bias[:, 0:256] = jnp.where(lane < 224, t32[0:1], zero)
    bias[:, 256:512] = t64[1:2]
    bias[:, 512:768] = t64[1:2]
    bias[:, 768:896] = jnp.where(lane < 64, t64[1:2], zero)[:, 0:128]
    bias[:, 896:1152] = t64[2:3]
    bias[:, 1152:1408] = jnp.where(lane < 192, t64[2:3], zero)
    wide = pack[...].astype(F32)
    for k in range(5):
        bias[:, 1408 + 128 * k:1536 + 128 * k] = wide[3 + k:4 + k]


def prepare_heads(value, advantage, legal, stage, head_w, legal_t):
    stage[...] = jnp.zeros_like(stage)
    stage[0:ACTIONS, :] = advantage[...].astype(F32)
    stage[ACTIONS:ACTIONS + 1, :] = value[...].astype(F32)
    head_w[...] = stage[...].astype(BF)
    stage[...] = jnp.zeros_like(stage)
    stage[0:ACTIONS, 0:legal.shape[1]] = legal[...].astype(F32)
    row = iota((128, 128), 0)
    legal_t[...] = jnp.where(row == 0, 1.0, stage[:, 0:128]).astype(BF)


def prepare_meta(act, game, ret, boot, weight, index, count, stage, meta_out):
    cap, peers = act.shape
    stage[:, 0:128] = jnp.zeros((128, 128), F32)
    fields = (
        act[...].astype(F32),
        game[...].astype(F32),
        ret[...] + GAMMA_THREE * boot[...],
        weight[...],
        index[...].astype(F32),
        (iota((cap, peers), 0) < count[...]).astype(F32),
    )
    for k, field in enumerate(fields):
        stage[8 * k:8 * k + cap, 0:peers] = field
    by_peer = stage[:, 0:128].T
    rows = 8 * peers
    repeat = (iota((rows, 128), 1) == iota((rows, 128), 0) // 8).astype(F32).astype(BF)
    spread = sum(dot(repeat, part) for part in split3(by_peer))
    spread = jnp.where(iota((rows, 128), 0) % 8 == iota((rows, 128), 1) % 8, spread, 0.0)
    collect = (iota((128, 128), 0) // 8 == iota((128, 128), 1)).astype(F32).astype(BF)
    meta_out[...] = sum(dot(part, collect) for part in split3(spread))


def learner_kernel(
    sizes,
    x_in, act, game, ret, boot, weight, index, count, table, legal, w1, w2, w3, r1, r2, r3, r4, rv, ra, value, advantage,
    dense_in,
    dg_out, sp_out, lp_out, q_out, tab_out,
    x_buf, x3, a1, s1, a2, s2, a3, s3, g3, g2, dw, t1, t2a, t2b, t2c, t3a, t3b, u2, u3, acc,
    bias, stage, pack, head_w, legal_t, meta_out, meta_in, q_send, q_in, a3t, a_in, g4_send, g4_in,
    part, codes, z_in, dg, sp, sp_in, sp_mid, sp_z, sp_all, lp, lp_in, lp_mid, lp_z, lp_all,
    x_sem, dw_sem, out_sem, leave_sem, join_sem, act_sem, act_core_sem, z_sem, near_sem, diag_sem,
):
    hsize, dsize, zrows = sizes
    zsize = dsize // 2
    peers = hsize * dsize
    region = sum(zrows) * (zsize // 2)
    group, share = small_group(sizes)
    h = lax.axis_index("hst")
    d = lax.axis_index("dev")
    z = d // 2
    core = d % 2
    mine = 2 * h + core
    me = h * dsize + d

    def where_is(peer):
        return (peer // dsize, peer % dsize)

    arrive = {
        "act": act_sem, "act_core": act_core_sem, "gather_z": z_sem, "gather_near": near_sem, "gather_diag": diag_sem,
    }

    def transfer(kind, at, src, dst, device):
        leave = leave_sem.at[LEAVE.index(kind if kind in LEAVE else kind + str(at[0]))]
        if kind in arrive:
            join = arrive[kind].at[at]
        else:
            join = join_sem.at[JOIN.index(kind if kind in JOIN else kind + str(at[0]))]
        return pltpu.make_async_remote_copy(
            src_ref=src, dst_ref=dst, send_sem=leave, recv_sem=join, device_id=device, device_id_type=MESH
        )

    def send(kind, at, src, dst, device):
        transfer(kind, at, src, dst, device).start()

    def landed(kind, at, dst):
        transfer(kind, at, dst, dst, (h, d)).wait_recv()

    def sent(kind, at, src):
        transfer(kind, at, src, src, (h, d)).wait_send()

    def fetch(c, slot, count=PIXELS):
        return pltpu.make_async_copy(
            x_in.at[pl.ds(pl.multiple_of(PIXELS * c, 16), count)], x_buf.at[slot, pl.ds(0, count)], x_sem.at[slot]
        )

    last = h >= 0

    @pl.when(last)
    def _():
        for c in range(SLOTS):
            fetch(c, c).start()
        barrier = pltpu.get_barrier_semaphore()

        def greet(k, carry):
            pl.semaphore_signal(barrier, inc=1, device_id=where_is((me + k) % peers), device_id_type=MESH)
            return carry

        lax.fori_loop(1, peers, greet, 0)
        pltpu.make_async_copy(dense_in, dw.at[pl.ds(0, FLAT)], dw_sem).start()
        dw[pl.ds(FLAT, 64)] = jnp.zeros((64, HIDDEN), BF)
        build_toeplitz(w1, w2, w3, t1, t2a, t2b, t2c, t3a, t3b)

    @pl.when(last)
    def _():
        expand_bias((r1, r2, r3, r4, rv, ra), stage, pack, bias)
        prepare_heads(value, advantage, legal, stage, head_w, legal_t)
        prepare_meta(act, game, ret, boot, weight, index, count, stage, meta_out)

    def chunk(c, carry):
        slot = c % SLOTS
        fetch(c, slot).wait()
        relayout(x_buf.at[slot], x3, 8 * c + 4)

        @pl.when(c + SLOTS < CHUNKS - 1)
        def _():
            fetch(c + SLOTS, slot).start()

        @pl.when(c + SLOTS == CHUNKS - 1)
        def _():
            fetch(CHUNKS - 1, slot, PIXELS // 2).start()

        conv1_rows(c, x3, t1, bias, a1, s1)
        return carry

    lax.fori_loop(0, 4, chunk, 0)

    @pl.when(last)
    def _():
        pl.semaphore_wait(pltpu.get_barrier_semaphore(), peers - 1)

        def give(k, carry):
            peer = (me + k) % peers
            send(
                "meta", k, meta_out.at[pl.ds(pl.multiple_of(8 * peer, 8), 8)],
                meta_in.at[pl.ds(pl.multiple_of(8 * me, 8), 8)], where_is(peer),
            )
            return carry

        lax.fori_loop(1, peers, give, 0)

    lax.fori_loop(4, CHUNKS - 1, chunk, 0)

    @pl.when(last)
    def _():
        slot = (CHUNKS - 1) % SLOTS
        fetch(CHUNKS - 1, slot, PIXELS // 2).wait()
        relayout(x_buf.at[slot], x3, 8 * (CHUNKS - 1) + 4, 4)
        conv1_rows(CHUNKS - 1, x3, t1, bias, a1, s1, (0,))

    sibling = (h, 2 * z + 1 - core)
    row_me = pl.ds(pl.multiple_of(8 * me, 8), 8)
    hy, hx = h // 2, h % 2
    flip_x, flip_y = 2 * hy + 1 - hx, 2 * (1 - hy) + hx
    near = (1 - core) * flip_x + core * flip_y
    far = (1 - core) * flip_y + core * flip_x
    across = 3 - h

    def plane(j):
        return (j // 2, 2 * z + j % 2)

    def features(f, to):
        return a3t.at[pl.ds(pl.multiple_of(784 * to + START[f], 16), ROWS[f])]

    def received(f, src):
        return a_in.at[src, pl.ds(ROWS[0] * f, ROWS[f])]

    def send_features(f):
        for k in range(1, hsize):
            to = (h + k) % hsize
            send("act", (f, k), features(f, to), received(f, mine), (to, d))
        send("act_core", (f, 0), features(f, h), received(f, mine), sibling)

    def forward_features(f):
        for k in range(1, hsize):
            src = 2 * ((h - k + hsize) % hsize) + core
            landed("act", (f, k), received(f, src))
            send("act_core", (f, k), received(f, src), received(f, src), sibling)

    def partial(f):
        for k in range(hsize):
            src = 2 * ((h - k + hsize) % hsize) + 1 - core
            landed("act_core", (f, k), received(f, src))
        if f == 0:
            landed("g4", 0, g4_in.at[pl.ds(0, 2 * hsize - 1)])
        left = jnp.concatenate([received(f, j)[...] for j in range(2 * hsize)], 1)
        right = jnp.concatenate([g4_in[j] for j in range(2 * hsize)], 0)
        product = dot(left, right)
        n = zrows[f]
        spare = jnp.zeros((n * (zsize // 2) - ROWS[f], 128), F32)
        for lanes in range(2):
            column = product[:, 128 * lanes:128 * lanes + 128]
            if spare.shape[0]:
                column = jnp.concatenate([column, spare], 0)
            for j in range(zsize // 2):
                chunk = column[n * j:n * j + n]
                part[f, 2 * j + lanes, 0:n] = chunk
                codes[f, 2 * j + lanes, 0:n], codes[f, 2 * j + lanes, n:n + 16] = to_fixed(chunk)
        for k in range(1, zsize):
            to = (z + k) % zsize
            send("sum", (f, k), codes.at[f, to, pl.ds(0, n + 16)], z_in.at[f, z, pl.ds(0, n + 16)], (h, 2 * to + core))

    def corner(f, hh, zz, cc):
        rows = region * hh + zrows[0] * (zsize // 2) * f + zrows[f] * (zz // 2)
        return pl.multiple_of(rows, 16), pl.multiple_of(256 * cc + 128 * (zz % 2), 128)

    def place(f, hh, zz, cc):
        rows, lanes = corner(f, hh, zz, cc)
        return dg.at[pl.ds(rows, zrows[f]), pl.ds(lanes, 128)]

    def spread(f, zz, k):
        at = place(f, h, zz, core)
        send("gather_near", (f, 0, k), at, at, (near, d))
        send("gather_near", (f, 1, k), at, at, (far, d))
        send("gather_core", (f, 0, k), at, at, sibling)

    def finish(f):
        n = zrows[f]
        landed("sum", (f, 0), z_in.at[f, pl.ds(0, zsize - 1), pl.ds(0, n + 16)])
        total = part[f, z, 0:n]
        for k in range(1, zsize):
            src = (z - k + zsize) % zsize
            total = total + from_fixed(z_in[f, src, 0:n], z_in[f, src, n:n + 16])
        rows, lanes = corner(f, h, z, core)
        dg[pl.ds(rows, n), pl.ds(lanes, 128)] = total.astype(BF)
        at = place(f, h, z, core)
        for k in range(1, zsize):
            send("gather_z", (f, k), at, at, (h, 2 * ((z + k) % zsize) + core))
        spread(f, z, 0)

    def pass_on(f):
        for k in range(1, zsize):
            zz = (z - k + zsize) % zsize
            landed("gather_z", (f, k), place(f, h, zz, core))
            spread(f, zz, k)

    def pass_across(f, first=0, count=99):
        for k in range(first, min(first + count, zsize)):
            zz = (z - k + zsize) % zsize
            at = place(f, near, zz, core)
            landed("gather_near", (f, 0, k), at)
            send("gather_diag", (f, k), at, at, (far, d))
            send("gather_core", (f, 1, k), at, at, sibling)
            at = place(f, far, zz, core)
            landed("gather_near", (f, 1, k), at)
            send("gather_core", (f, 2, k), at, at, sibling)

    def pass_last(f):
        for k in range(zsize):
            at = place(f, across, (z - k + zsize) % zsize, core)
            landed("gather_diag", (f, k), at)
            send("gather_core", (f, 3, k), at, at, sibling)

    def gather_core(f):
        landed("gather_core", (f, 0), dg.at[pl.ds(0, zrows[f] * zsize)])

    def group_rows(j):
        return pl.ds(pl.multiple_of(group * j, 8), group)

    def share_rows(j, zz):
        return pl.ds(pl.multiple_of(group * j + share * zz, 8), share)

    def small_send():
        for k in range(1, 2 * hsize):
            to = (mine + k) % (2 * hsize)
            send("small", k, sp.at[group_rows(to)], sp_in.at[mine], plane(to))
        sp_in[mine] = sp[group_rows(mine), :]

    def small_sum():
        landed("small", 0, sp_in.at[pl.ds(0, 2 * hsize - 1)])
        total = sp_in[0]
        for j in range(1, 2 * hsize):
            total = total + sp_in[j]
        sp_mid[...] = total
        for k in range(1, zsize):
            to = (z + k) % zsize
            send("small_z", k, sp_mid.at[pl.ds(pl.multiple_of(share * to, 8), share)], sp_z.at[z], (h, 2 * to + core))
        sp_z[z] = sp_mid[pl.ds(pl.multiple_of(share * z, 8), share), :]

    def small_finish():
        landed("small_z", 0, sp_z.at[pl.ds(0, zsize - 1)])
        total = sp_z[0]
        for j in range(1, zsize):
            total = total + sp_z[j]
        sp_all[share_rows(mine, z), :] = total
        at = sp_all.at[share_rows(mine, z)]
        for k in range(1, zsize):
            send("small_back", k, at, at, (h, 2 * ((z + k) % zsize) + core))

    def small_spread():
        landed("small_back", 0, sp_z.at[pl.ds(0, zsize - 1)])
        at = sp_all.at[group_rows(mine)]
        for k in range(1, hsize):
            send("small_all", k, at, at, ((h + k) % hsize, d))
        send("small_core", 0, at, at, sibling)

    def small_share():
        landed("small_all", 0, sp_in.at[pl.ds(0, hsize - 1)])
        for k in range(1, hsize):
            at = sp_all.at[group_rows(2 * ((h - k + hsize) % hsize) + core)]
            send("small_core", k, at, at, sibling)

    def late_rows(j):
        return pl.ds(pl.multiple_of(16 * j, 16), 16)

    def late_send():
        for k in range(1, 2 * hsize):
            to = (mine + k) % (2 * hsize)
            send("late", k, lp.at[late_rows(to)], lp_in.at[mine], plane(to))
        lp_in[mine] = lp[late_rows(mine), :]

    def late_sum():
        landed("late", 0, lp_in.at[pl.ds(0, 2 * hsize - 1)])
        total = lp_in[0]
        for j in range(1, 2 * hsize):
            total = total + lp_in[j]
        lp_mid[...] = total
        lp_z[z] = total
        for k in range(1, zsize):
            send("late_z", k, lp_mid, lp_z.at[z], (h, 2 * ((z + k) % zsize) + core))

    def late_spread():
        landed("late_z", 0, lp_z.at[pl.ds(0, zsize - 1)])
        total = lp_z[0]
        for j in range(1, zsize):
            total = total + lp_z[j]
        lp_all[late_rows(mine), :] = total
        at = lp_all.at[late_rows(mine)]
        for k in range(1, 2 * hsize):
            send("late_all", k, at, at, plane((mine + k) % (2 * hsize)))

    def dense_out(f):
        first, count = zrows[0] * (zsize // 2) * f, zrows[f] * (zsize // 2)
        return [
            pltpu.make_async_copy(
                dg.at[pl.ds(region * j + first, count)], dg_out.at[pl.ds(region * j + first, count)],
                out_sem.at[hsize * f + j],
            )
            for j in range(hsize)
        ]

    @pl.when(last)
    def _():
        conv2_all(a1, t2a, t2b, t2c, bias, a2, s2)
        conv3_all(a2, t3a, t3b, bias, a3, s3)
        for r in range(7):
            a3t[pl.ds(448 * r, 448), :] = a3[r].T[0:448]
        send_features(0)

    @pl.when(last)
    def _():
        pltpu.make_async_copy(dense_in, dw.at[pl.ds(0, FLAT)], dw_sem).wait()
        act4, slope4, head = dense_head(a3, dw, head_w, bias)

        landed("meta", 0, meta_in.at[pl.ds(0, 8 * (peers - 1))])
        meta_in[row_me, :] = meta_out[row_me, :]
        q, grow, dhb, loss, newt, top = td_part(
            head, meta_in[...], meta_out[...], legal_t[...], table[...], 8 * peers, float(peers * act.shape[0])
        )
        g4, dhw = head_grads(grow, act4, slope4, head_w)
        for half in range(2):
            g4_send[half] = g4[:, 256 * half:256 * half + 256]
        for k in range(1, 2 * hsize):
            to = (mine + k) % (2 * hsize)
            send("g4", k, g4_send.at[to % 2], g4_in.at[mine], plane(to))
        send_features(1)
        g4_in[mine] = g4_send[core]
        for f in range(2):
            received(f, mine)[...] = features(f, h)[...]
        tab_out[...] = jnp.broadcast_to(newt, (8, 128))
        lane = iota((8 * peers, 128), 1)
        q_send[...] = jnp.where(lane == 19, top, jnp.where(lane == 20, loss, q))
        for k in range(4):
            sp[pl.ds(640 + 24 * k, 24), :] = dhw[0:24, 128 * k:128 * k + 128]
        b4 = jnp.sum(g4.astype(F32), 0, keepdims=True)
        for k in range(4):
            sp[738 + k:739 + k, :] = b4[:, 128 * k:128 * k + 128]
        sp[742:743, :] = dhb
        sp[743:2 * hsize * group, :] = jnp.zeros((2 * hsize * group - 743, 128), F32)
        lp[64:, :] = jnp.zeros((lp.shape[0] - 64, 128), F32)
        sp[737:738, :] = fold64(g3_all(g4, dw, s3, g3))

    @pl.when(last)
    def _():
        build_transposed(w2, w3, u2, u3)

    @pl.when(last)
    def _():
        sp[736:737, :] = fold64(conv3_dx(g3, u3, s2, g2))
        forward_features(0)

    @pl.when(last)
    def _():
        conv3_dw(a2, g3, sp, 256)

    @pl.when(last)
    def _():
        conv2_dw(a1, g2, sp, 0, 0, 4)

    @pl.when(last)
    def _():
        partial(0)
        small_send()

    @pl.when(last)
    def _():
        stage[0:1, 0:256] = conv2_dx(g2, u2, s1, a1, 0, 2)
        forward_features(1)

    @pl.when(last)
    def _():
        b1 = conv2_dx(g2, u2, s1, a1, 2, 4) + stage[0:1, 0:256]
        b1 = b1[:, 0:128] + b1[:, 128:256]
        b1 = b1 + pltpu.roll(b1, 64, 1)
        lp[64:65, :] = b1 + pltpu.roll(b1, 32, 1)

    @pl.when(last)
    def _():
        partial(1)

    @pl.when(last)
    def _():
        conv1_dw(x3, a1, acc, 0, 2)

    @pl.when(last)
    def _():
        small_sum()
        finish(0)

    @pl.when(last)
    def _():
        conv1_dw(x3, a1, acc, 2, 5)

    @pl.when(last)
    def _():
        conv1_fold(acc, lp, 0)
        late_send()
        small_finish()
        pass_on(0)
        finish(1)
        late_sum()
        small_spread()
        pass_across(0)
        pass_on(1)

        def answer(k, carry):
            peer = (me + k) % peers
            send(
                "q", k, q_send.at[pl.ds(pl.multiple_of(8 * peer, 8), 8)],
                q_in.at[pl.ds(pl.multiple_of(8 * me, 8), 8)], where_is(peer),
            )
            return carry

        lax.fori_loop(1, peers, answer, 0)
        q_in[row_me, :] = q_send[row_me, :]

        pass_last(0)
        pass_across(1, 0, 2)
        late_spread()
        gather_core(0)
        first_half = dense_out(0)
        for copy in first_half:
            copy.start()
        pass_across(1, 2, zsize)
        small_share()
        pass_last(1)
        landed("small_core", 0, sp_in.at[pl.ds(0, hsize)])
        landed("late_all", 0, lp_in.at[pl.ds(0, 2 * hsize - 1)])

        landed("q", 0, q_in.at[pl.ds(0, 8 * (peers - 1))])
        others = [
            pltpu.make_async_copy(src, dst, out_sem.at[2 * hsize + k])
            for k, (src, dst) in enumerate(((sp_all, sp_out), (lp_all, lp_out), (q_in, q_out)))
        ]
        for copy in others:
            copy.start()
        gather_core(1)
        second_half = dense_out(1)
        for copy in second_half:
            copy.start()

        sent("meta", 0, meta_in.at[pl.ds(0, 8 * (peers - 1))])
        sent("q", 0, q_in.at[pl.ds(0, 8 * (peers - 1))])
        sent("act", (0, 0), a_in.at[pl.ds(0, hsize - 1)])
        sent("act_core", (0, 0), a_in.at[pl.ds(0, hsize)])
        sent("g4", 0, g4_in.at[pl.ds(0, 2 * hsize - 1)])
        sent("small", 0, sp_in.at[pl.ds(0, 2 * hsize - 1)])
        sent("small_z", 0, sp_z.at[pl.ds(0, zsize - 1)])
        sent("small_back", 0, sp_z.at[pl.ds(0, zsize - 1)])
        sent("small_all", 0, sp_in.at[pl.ds(0, hsize - 1)])
        sent("small_core", 0, sp_in.at[pl.ds(0, hsize)])
        sent("late", 0, lp_in.at[pl.ds(0, 2 * hsize - 1)])
        sent("late_z", 0, lp_z.at[pl.ds(0, zsize - 1)])
        sent("late_all", 0, lp_in.at[pl.ds(0, 2 * hsize - 1)])
        for f in range(2):
            n = zrows[f]
            sent("sum", (f, 0), z_in.at[f, pl.ds(0, zsize - 1), pl.ds(0, n + 16)])
            sent("gather_z", (f, 0), dg.at[pl.ds(0, n * (zsize - 1)), pl.ds(0, 128)])
            sent("gather_near", (f, 0, 0), dg.at[pl.ds(0, n * zsize), pl.ds(0, 256)])
            sent("gather_diag", (f, 0), dg.at[pl.ds(0, n * zsize), pl.ds(0, 128)])
            sent("gather_core", (f, 0), dg.at[pl.ds(0, n * zsize)])
        for copy in first_half + others + second_half:
            copy.wait()


def small_group(sizes):
    hsize, dsize, _ = sizes
    zsize = dsize // 2
    group = -(-743 // (2 * hsize * 8 * zsize)) * 8 * zsize
    return group, group // zsize


def learner(sizes, args, cap):
    hsize, dsize, zrows = sizes
    zsize, peers = dsize // 2, hsize * dsize
    region = sum(zrows) * (zsize // 2)
    group, share = small_group(sizes)
    dma = pltpu.SemaphoreType.DMA
    vmem = pltpu.VMEM
    groups = 2 * hsize
    scratch = [
        vmem((SLOTS, PIXELS, 128), BF), vmem((88, 128, 384), BF), vmem((21, 128, 768), BF), vmem((21, 128, 768), F32), vmem((9, 128, 640), BF),
        vmem((9, 128, 640), F32), vmem((7, 128, 512), BF), vmem((7, 128, 512), F32), vmem((11, 128, 512), BF),
        vmem((11, 128, 640), BF), vmem((3200, 512), BF), vmem((1024, 256), BF), vmem((2048, 256), BF),
        vmem((2048, 256), BF), vmem((1024, 128), BF), vmem((1536, 256), BF), vmem((1152, 256), BF),
        vmem((2, 2304, 256), BF), vmem((3072, 256), BF), vmem((256, 1024), F32),
        vmem((1, 2048), F32), vmem((128, 512), F32), vmem((8, 128), BF), vmem((128, 512), BF), vmem((128, 128), BF),
        vmem((8 * peers, 128), F32), vmem((8 * peers, 128), F32), vmem((8 * peers, 128), F32),
        vmem((8 * peers, 128), F32), vmem((FLAT, 128), BF), vmem((groups, sum(ROWS), 128), BF), vmem((2, 128, 256), BF),
        vmem((groups, 128, 256), BF), vmem((2, zsize, max(zrows), 128), F32), vmem((2, zsize, max(zrows) + 16, 128), jnp.int16),
        vmem((2, zsize, max(zrows) + 16, 128), jnp.int16), vmem((hsize * region, 512), BF),
        vmem((groups * group, 128), F32), vmem((groups, group, 128), F32), vmem((group, 128), F32),
        vmem((zsize, share, 128), F32), vmem((groups * group, 128), F32),
        vmem((16 * groups, 128), F32), vmem((groups, 16, 128), F32), vmem((16, 128), F32), vmem((zsize, 16, 128), F32),
        vmem((16 * groups, 128), F32),
        dma((SLOTS,)), dma, dma((2 * hsize + 3,)), dma((len(LEAVE),)), dma((len(JOIN),)),
        dma((2, hsize)), dma((2, hsize)), dma((2, zsize)), dma((2, 2, zsize)), dma((2, zsize)),
    ]
    whole = pl.BlockSpec(memory_space=pltpu.VMEM)
    outside = pl.BlockSpec(memory_space=pl.ANY)
    return pl.pallas_call(
        functools.partial(learner_kernel, sizes),
        in_specs=[outside] + [whole] * 20 + [outside],
        out_specs=[outside, outside, outside, outside, whole],
        out_shape=[
            jax.ShapeDtypeStruct((hsize * region, 512), BF),
            jax.ShapeDtypeStruct((groups * group, 128), F32),
            jax.ShapeDtypeStruct((16 * groups, 128), F32),
            jax.ShapeDtypeStruct((8 * peers, 128), F32),
            jax.ShapeDtypeStruct((8, 128), F32),
        ],
        scratch_shapes=scratch,
        compiler_params=pltpu.CompilerParams(collective_id=0, has_side_effects=True, vmem_limit_bytes=63 << 20),
    )(*args)


def output_kernel(
    hsize, region, second, dg, sp, lp, q, tab,
    dense, c1, c2, c3, bias1, bias2, bias3, bias4, vw, vb, aw, ab, loss, top, table, qt,
    held, wide, in_sem, out_sem,
):
    reads = []
    for j in range(2 * hsize):
        f = j % 2
        src, at, count = region * (j // 2) + f * (second + 16), 784 * (j // 2) + f * ROWS[0], ROWS[f] - 16 * f
        copy = pltpu.make_async_copy(dg.at[pl.ds(src, count)], held.at[pl.ds(at, count)], in_sem.at[j])
        reads.append((copy, at, count))
    for copy, _, _ in reads:
        copy.start()
    for a in range(2):
        c1[pl.ds(128 * a, 128), :] = lp[pl.ds(32 * a, 32), :].T
    for kr in range(4):
        c2[pl.ds(128 * kr, 128), :] = sp[pl.ds(64 * kr, 64), :].T
    for kr in range(3):
        c3[pl.ds(192 * kr, 128), :] = sp[pl.ds(256 + 128 * kr, 64), :].T
        c3[pl.ds(192 * kr + 128, 64), :] = sp[pl.ds(320 + 128 * kr, 64), :].T[0:64]
    bias1[...] = lp[64:65, 0:32]
    bias2[...] = sp[736:737, 0:64]
    bias3[...] = sp[737:738, 0:64]
    for k in range(4):
        bias4[:, 128 * k:128 * k + 128] = sp[738 + k:739 + k, :]
        heads = sp[pl.ds(640 + 24 * k, 24), :]
        aw[:, 128 * k:128 * k + 128] = heads[0:ACTIONS]
        vw[:, 128 * k:128 * k + 128] = heads[ACTIONS:ACTIONS + 1]
    ab[...] = sp[742:743, 0:ACTIONS]
    vb[...] = sp[742:743, ACTIONS:ACTIONS + 1]
    rows = q[...]
    top[...] = jnp.max(rows[:, 19:20], 0, keepdims=True)
    first = iota((rows.shape[0], 1), 0) % 8 == 0
    loss[...] = jnp.sum(jnp.where(first, rows[:, 20:21], 0.0), 0, keepdims=True)
    table[...] = tab[0:1, :]
    turned = rows.T
    for k in range(ACTIONS):
        qt[k] = turned[k:k + 1]
    writes = []
    for j, (copy, at, count) in enumerate(reads):
        copy.wait()
        wide[pl.ds(at, count)] = held[pl.ds(at, count)].astype(F32)
        writes.append(pltpu.make_async_copy(wide.at[pl.ds(at, count)], dense.at[pl.ds(at, count)], out_sem.at[j]))
        writes[-1].start()
    for copy in writes:
        copy.wait()


def outputs(sizes, dg, sp, lp, q, tab):
    hsize, dsize, zrows = sizes
    region, second = sum(zrows) * (dsize // 4), zrows[0] * (dsize // 4)
    whole = pl.BlockSpec(memory_space=pltpu.VMEM)
    outside = pl.BlockSpec(memory_space=pl.ANY)
    shapes = (
        (FLAT, 512), (256, 32), (512, 64), (576, 64), (1, 32), (1, 64), (1, 64), (1, 512), (1, 512), (1, 1),
        (ACTIONS, 512), (1, ACTIONS), (1, 1), (1, 1), (1, 128), (ACTIONS, 1, 8 * hsize * dsize),
    )
    return pl.pallas_call(
        functools.partial(output_kernel, hsize, region, second),
        in_specs=[outside, whole, whole, whole, whole],
        out_specs=[outside] + [whole] * 15,
        out_shape=[jax.ShapeDtypeStruct(s, F32) for s in shapes],
        scratch_shapes=[
            pltpu.VMEM((FLAT, 512), BF), pltpu.VMEM((FLAT, 512), F32),
            pltpu.SemaphoreType.DMA((2 * hsize,)), pltpu.SemaphoreType.DMA((2 * hsize,)),
        ],
        compiler_params=pltpu.CompilerParams(vmem_limit_bytes=63 << 20),
    )(dg, sp, lp, q, tab)


def per_device(
    hsize,
    dsize,
    replay,
    send_index,
    send_count,
    actions,
    game_ids,
    legal_table,
    returns,
    bootstrap,
    is_weights,
    priority_table,
    conv1_w,
    conv1_b,
    conv2_w,
    conv2_b,
    conv3_w,
    conv3_b,
    dense_w,
    dense_b,
    value_w,
    value_b,
    advantage_w,
    advantage_b,
):
    cap = send_index.shape[2]
    peers = hsize * dsize
    zsize = dsize // 2
    zrows = tuple(-(-rows // (8 * zsize)) * 16 for rows in ROWS)
    sizes = (hsize, dsize, zrows)
    args = (
        replay.T,
        actions[0].T,
        game_ids[0].T,
        returns[0].T,
        bootstrap[0].T,
        is_weights[0].T,
        send_index[0].T,
        send_count,
        priority_table.reshape(1, -1),
        legal_table.T,
        conv1_w.reshape(256, 32),
        conv2_w.reshape(512, 64),
        conv3_w.reshape(576, 64),
        conv1_b.reshape(1, -1),
        conv2_b.reshape(1, -1),
        conv3_b.reshape(1, -1),
        dense_b.reshape(4, -1),
        value_b.reshape(1, -1),
        advantage_b.reshape(1, -1),
        value_w.T,
        advantage_w.T,
        dense_w,
    )
    dg, sp, lp, q, tab = learner(sizes, args, cap)
    (dense, c1, c2, c3, b1, b2, b3, b4, vw, vb, aw, ab, loss, top, table, qt) = outputs(sizes, dg, sp, lp, q, tab)
    q_values = qt.transpose(1, 2, 0)
    if cap != 8:
        q_values = q_values.reshape(1, peers, 8, ACTIONS)[:, :, :cap].reshape(1, peers * cap, ACTIONS)
    return (
        q_values,
        loss.reshape(()),
        c1.reshape(conv1_w.shape),
        b1.reshape(-1),
        c2.reshape(conv2_w.shape),
        b2.reshape(-1),
        c3.reshape(conv3_w.shape),
        b3.reshape(-1),
        dense,
        b4.reshape(-1),
        vw.T,
        vb.reshape(-1),
        aw.T,
        ab.reshape(-1),
        table.reshape(-1),
        top.reshape(()),
    )


def solution(mesh):
    both = ("hst", "dev")
    rows2, rows3 = P(both, None), P(both, None, None)
    placed = (rows2, rows3, rows2, rows3, rows3, P(), rows3, rows3, rows3, P(both)) + (P(),) * 12
    return jax.shard_map(
        functools.partial(per_device, mesh.shape["hst"], mesh.shape["dev"]),
        mesh=mesh,
        in_specs=placed,
        out_specs=(rows3,) + (P(),) * 13 + (P(both), P()),
        check_vma=False,
    )
```

time: 105 us -> 77.7 us (0.74)
  Pallas kernels: 97.8 us -> 76.1 us
  local copies, waits for them, and re-layouts: 5.64 us -> 0 us
    pallas_call x2, Pallas kernels: 97.8 us -> 76.1 us  [the longest x1 70.2 us: learner(): pl.pallas_call(functools.partial(learner_kernel, sizes), in_specs=[outsid...]
    concatenate x1 -> x0, local copies, waits for them, and re-layouts: 4.03 us -> none  [per_device(): jnp.concatenate([conv1_b, gap(96), conv2_b, gap(64), conv3_b, gap(64), de...]
where the time goes in v3:
time: 77.7 us; the launch traced here: 77.5 us
  Pallas kernels  76.1 us (98%)
  between operations  1.5 us (2%)
    pallas_call x1, Pallas kernels, learner(): pl.pallas_call(functools.partial(learner_kernel, sizes), in_specs=[outsid...  70.2 us
    pallas_call x1, Pallas kernels, outputs(): pl.pallas_call(functools.partial(output_kernel, hsize, region, second), i...  5.89 us

profile of v3, /device:TPU:1, one launch (start us, length us, event | category | flops | bytes accessed | tf_op | source)
XLA Modules:
  0.0 77.5 jit_solution(11305659844156498439)
XLA Ops:
  1.3 70.2 %shard_map.333 = (bf16[3200,512]{1,0:T(8,128)(2,1)}, f32[768,128]{1,0:T(8,128)}, f32[128,128]{1,0:T(8,128)}, f32[256,128]{1,0:T(8,128)}, f32[8,128]{1,0:T(8,128)}) custom-call(bf16[28224,128]{1,0:T(8,128)(2,1)} %bitcast.48, s32[8,32]{1,0:T(8,128)} %bitcast.54, s32[8,32]{1,0:T(8,128)} %bitcast.55, f32[8,32]{1,0:T(8,128)} %bitcast.56, f32[8,32]{1,0:T(8,128)} %bitcast.57, ...), custom_call_target="tpu_custom_call" | custom-call | tf_op jit(solution)/shard_map/pallas_call | solution.py:932
  71.5 5.9 %shard_map.334 = (f32[3136,512]{1,0:T(8,128)}, f32[256,32]{1,0:T(8,128)}, f32[512,64]{1,0:T(8,128)}, f32[576,64]{1,0:T(8,128)}, f32[1,32]{1,0:T(1,128)}, /*index...) custom-call(bf16[3200,512]{1,0:T(8,128)(2,1)} %get-tuple-element.37., ...), custom_call_target="tpu_custom_call" | custom-call | tf_op jit(solution)/shard_map/pallas_call | solution.py:1005

commit v4 on v3

--- a/solution.py
+++ b/solution.py
@@ -503,6 +503,8 @@
         fetch(c, slot).wait()
         relayout(x_buf.at[slot], x3, 8 * c + 4)
 
+        conv1_rows(c, x3, t1, bias, a1, s1)
+
         @pl.when(c + SLOTS < CHUNKS - 1)
         def _():
             fetch(c + SLOTS, slot).start()
@@ -511,7 +513,6 @@
         def _():
             fetch(CHUNKS - 1, slot, PIXELS // 2).start()
 
-        conv1_rows(c, x3, t1, bias, a1, s1)
         return carry
 
     lax.fori_loop(0, 4, chunk, 0)
@@ -720,12 +721,13 @@
         for k in range(1, 2 * hsize):
             send("late_all", k, at, at, plane((mine + k) % (2 * hsize)))
 
-    def dense_out(f):
+    def dense_out(f, cc, at):
         first, count = zrows[0] * (zsize // 2) * f, zrows[f] * (zsize // 2)
+        lanes = pl.ds(pl.multiple_of(256 * cc, 128), 256)
         return [
             pltpu.make_async_copy(
-                dg.at[pl.ds(region * j + first, count)], dg_out.at[pl.ds(region * j + first, count)],
-                out_sem.at[hsize * f + j],
+                dg.at[pl.ds(region * j + first, count), lanes], dg_out.at[pl.ds(region * j + first, count), lanes],
+                out_sem.at[hsize * (2 * f + at) + j],
             )
             for j in range(hsize)
         ]
@@ -849,7 +851,7 @@
         pass_across(1, 0, 2)
         late_spread()
         gather_core(0)
-        first_half = dense_out(0)
+        first_half = dense_out(0, core, 0) + dense_out(0, 1 - core, 1)
         for copy in first_half:
             copy.start()
         pass_across(1, 2, zsize)
@@ -860,14 +862,17 @@
 
         landed("q", 0, q_in.at[pl.ds(0, 8 * (peers - 1))])
         others = [
-            pltpu.make_async_copy(src, dst, out_sem.at[2 * hsize + k])
+            pltpu.make_async_copy(src, dst, out_sem.at[4 * hsize + k])
             for k, (src, dst) in enumerate(((sp_all, sp_out), (lp_all, lp_out), (q_in, q_out)))
         ]
         for copy in others:
             copy.start()
+        own_half = dense_out(1, core, 0)
+        for copy in own_half:
+            copy.start()
         gather_core(1)
-        second_half = dense_out(1)
-        for copy in second_half:
+        other_half = dense_out(1, 1 - core, 1)
+        for copy in other_half:
             copy.start()
 
         sent("meta", 0, meta_in.at[pl.ds(0, 8 * (peers - 1))])
@@ -890,7 +895,7 @@
             sent("gather_near", (f, 0, 0), dg.at[pl.ds(0, n * zsize), pl.ds(0, 256)])
             sent("gather_diag", (f, 0), dg.at[pl.ds(0, n * zsize), pl.ds(0, 128)])
             sent("gather_core", (f, 0), dg.at[pl.ds(0, n * zsize)])
-        for copy in first_half + others + second_half:
+        for copy in first_half + others + own_half + other_half:
             copy.wait()
 
 
@@ -924,7 +929,7 @@
         vmem((zsize, share, 128), F32), vmem((groups * group, 128), F32),
         vmem((16 * groups, 128), F32), vmem((groups, 16, 128), F32), vmem((16, 128), F32), vmem((zsize, 16, 128), F32),
         vmem((16 * groups, 128), F32),
-        dma((SLOTS,)), dma, dma((2 * hsize + 3,)), dma((len(LEAVE),)), dma((len(JOIN),)),
+        dma((SLOTS,)), dma, dma((4 * hsize + 3,)), dma((len(LEAVE),)), dma((len(JOIN),)),
         dma((2, hsize)), dma((2, hsize)), dma((2, zsize)), dma((2, 2, zsize)), dma((2, zsize)),
     ]
     whole = pl.BlockSpec(memory_space=pltpu.VMEM)

time: 77.7 us -> 77.6 us (level)
  no operation moved by 1% of the time
where the time goes in v4:
time: 77.6 us; the launch traced here: 77.4 us
  Pallas kernels  75.9 us (98%)
  between operations  1.5 us (2%)
    pallas_call x1, Pallas kernels, learner(): pl.pallas_call(functools.partial(learner_kernel, sizes), in_specs=[outsid...  70 us
    pallas_call x1, Pallas kernels, outputs(): pl.pallas_call(functools.partial(output_kernel, hsize, region, second), i...  5.89 us

profile of v4, /device:TPU:1, one launch (start us, length us, event | category | flops | bytes accessed | tf_op | source)
XLA Modules:
  0.0 77.4 jit_solution(6635041590686328231)
XLA Ops:
  1.3 70.0 %shard_map.333 = (bf16[3200,512]{1,0:T(8,128)(2,1)}, f32[768,128]{1,0:T(8,128)}, f32[128,128]{1,0:T(8,128)}, f32[256,128]{1,0:T(8,128)}, f32[8,128]{1,0:T(8,128)}) custom-call(bf16[28224,128]{1,0:T(8,128)(2,1)} %bitcast.48, s32[8,32]{1,0:T(8,128)} %bitcast.54, s32[8,32]{1,0:T(8,128)} %bitcast.55, f32[8,32]{1,0:T(8,128)} %bitcast.56, f32[8,32]{1,0:T(8,128)} %bitcast.57, ...), custom_call_target="tpu_custom_call" | custom-call | tf_op jit(solution)/shard_map/pallas_call | solution.py:937
  71.3 5.9 %shard_map.334 = (f32[3136,512]{1,0:T(8,128)}, f32[256,32]{1,0:T(8,128)}, f32[512,64]{1,0:T(8,128)}, f32[576,64]{1,0:T(8,128)}, f32[1,32]{1,0:T(1,128)}, /*index...) custom-call(bf16[3200,512]{1,0:T(8,128)(2,1)} %get-tuple-element.37., ...), custom_call_target="tpu_custom_call" | custom-call | tf_op jit(solution)/shard_map/pallas_call | solution.py:1010
